TPU v7x, 128 devices: a whole 4x4x4 slice. The times are simulated.
128 devices in a mesh: row: 8 (over z, core), col: 16 (over y, x).
Axes of the slice: x: 4, y: 4, z: 4, core: 2. Of those that a mesh axis runs over, the one named last changes fastest.
Arguments:
- single: bfloat16 [65536, 384], P(('row', 'col')), may hold values from -20 to 20
- left_weight: bfloat16 [384, 128], replicated, may hold values from -0.3125 to 0.3125
- right_weight: bfloat16 [384, 128], replicated, may hold values from -0.3125 to 0.3125
- bin_weight: bfloat16 [128, 64], replicated, may hold values from -3 to 3
- bin_bias: float32 [64], replicated, may hold values from -4 to 4
- block_tiles: int32 [128, 8, 2], P(('row', 'col')), may hold values from 0 to 511, as said below
- block_count: int32 [128], P(('row', 'col')), may hold values from 1 to 8, as said below
- teacher: bfloat16 [128, 8, 64, 128, 128], P(('row', 'col')), may hold values from 0 to 1, as said below
Outputs:
- grad_single: bfloat16 [65536, 384], P(('row', 'col'))
- grad_left: float32 [384, 128], replicated
- grad_right: float32 [384, 128], replicated
- grad_bin: float32 [128, 64], replicated
- loss: float32 [], replicated
Inputs may be any that keep to these rules, and one draw needn't show every extreme that they name: `block_tiles`: for the device at mesh position (r, c), with tile t held by device t // 4 in row-major mesh order, each slot's row tile is held by a device of mesh row r and its column tile by a device of mesh column c. Slots 2m and 2m + 1 take their row tiles from one device and their column tiles from one device; different m take them from different devices, so at most two slots of a device name tiles of any one device on each side. Slots from block_count on are ignored. `block_count`: counts differ from device to device; some device holds 8 kept blocks. `teacher`: each pair's probabilities over the bins are positive and sum to one up to bfloat16 rounding.
All inputs are finite; a program needn't handle non-finite values.
Results may differ from a plain program's by a relative error of at most 0.011.
Values may be sent and summed in bfloat16 or wider, within the bound.
No kernel may reach another device: no remote copies, remote signals or barrier semaphores. Data moves between devices by JAX's collectives and lax.ppermute only.
A program may use at most 64 MiB of HBM per device.

v0:
```python
import functools
import jax
import jax.numpy as jnp
from jax import lax
from jax.experimental import pallas as pl
from jax.experimental.pallas import tpu as pltpu
from jax.sharding import Mesh
from jax.sharding import PartitionSpec as P

GROUP_SCORES = 32
GROUP_SOFT = 16
GROUP_GRADS = 32


def blocks_kernel(
    place, count, bias, w_turned, w_plain, left0, left1, left2, left3, right0, right1, teacher,
    left_grads, right_grads, bin_out, cross_out,
    w_rows, w_wide, w_cols, left_tiles, right_tiles, target, logit, left_turn, right_turn, left_sum, right_sum,
    tile_sem, target_sem,
):
    left_from = (left0, left1, left2, left3)
    right_from = (right0, right1)
    slots, bins, tile, width = teacher.shape
    live = count[0]

    def target_copy(slot):
        return pltpu.make_async_copy(
            teacher.at[slot], target.at[lax.rem(slot, 2)], target_sem.at[lax.rem(slot, 2)]
        )

    def left_copy(slot, n):
        return pltpu.make_async_copy(
            left_from[n].at[slot], left_tiles.at[slot], tile_sem.at[slot, 0]
        )

    def right_copy(slot, n):
        return pltpu.make_async_copy(
            right_from[n].at[pl.ds(pl.multiple_of(place[slot, 2] * tile, tile), tile)],
            right_tiles.at[slot], tile_sem.at[slot, 1]
        )

    for slot in range(slots):
        for n in range(len(left_from)):

            @pl.when((slot < live) & (place[slot, 0] == n))
            def _():
                left_copy(slot, n).start()

        for n in range(len(right_from)):

            @pl.when((slot < live) & (place[slot, 1] == n))
            def _():
                right_copy(slot, n).start()

    target_copy(0).start()
    for k in range(bins):
        row = w_turned[k : k + 1, :]
        w_wide[k] = jnp.broadcast_to(row, (8, width))
        w_rows[k] = jnp.broadcast_to(row, (16, width)).astype(jnp.bfloat16)
        w_cols[k] = jnp.broadcast_to(w_plain[:, k : k + 1], (width, tile)).astype(jnp.bfloat16)
    bin_out[...] = jnp.zeros(bin_out.shape, jnp.float32)
    cross_out[...] = jnp.zeros(cross_out.shape, jnp.float32)

    def block(slot, _):
        buf = lax.rem(slot, 2)

        @pl.when(slot + 1 < live)
        def _():
            target_copy(slot + 1).start()

        left_copy(slot, 0).wait()
        right_copy(slot, 0).wait()
        left = left_tiles[slot]
        right = right_tiles[slot]
        left_turn[...] = left.T
        right_turn[...] = right.T
        left_sum[...] = jnp.zeros(left_sum.shape, jnp.float32)
        right_sum[...] = jnp.zeros(right_sum.shape, jnp.float32)

        def scores(g, highest):
            left = left_tiles[slot].reshape(tile // 16, 16, width)
            for j in range(GROUP_SCORES):
                k = g * GROUP_SCORES + j
                scaled = (left * w_rows[k][None]).reshape(tile, width)
                value = jnp.dot(scaled, right_turn[...], preferred_element_type=jnp.float32)
                value = value + bias[k]
                logit[k] = value
                highest = jnp.maximum(highest, value)
            return highest

        highest = lax.fori_loop(
            0, bins // GROUP_SCORES, scores, jnp.full((tile, tile), -jnp.inf, jnp.float32)
        )
        target_copy(slot).wait()

        STEP = 32
        ratios = []
        for p in range(0, tile, STEP):
            rows = pl.ds(p, STEP)
            top = highest[p : p + STEP]

            def soft(g, carried):
                total, mass, cross = carried
                for j in range(GROUP_SOFT):
                    k = g * GROUP_SOFT + j
                    value = logit[k, rows, :] - top
                    power = jnp.exp(value)
                    goal = target[buf, k, rows, :].astype(jnp.float32)
                    total = total + power
                    mass = mass + goal
                    cross = cross + goal * value
                    logit[k, rows, :] = power
                return total, mass, cross

            zero = jnp.zeros((STEP, tile), jnp.float32)
            total, mass, cross = lax.fori_loop(0, bins // GROUP_SOFT, soft, (zero, zero, zero))
            cross = mass * jnp.log(total) - cross
            cross_out[...] += cross.reshape(STEP // 8, 8, tile).sum(0)
            ratios.append(mass / total)
        ratio = jnp.concatenate(ratios, 0)

        def grads(g, _):
            left_wide = left_tiles[slot].astype(jnp.float32)
            pieces, scales = [], []
            left_part = jnp.zeros((tile, width), jnp.float32)
            for j in range(GROUP_GRADS):
                k = g * GROUP_GRADS + j
                grad = logit[k] * ratio - target[buf, k].astype(jnp.float32)
                grad = grad.astype(jnp.bfloat16)
                mixed = jnp.dot(grad, right_tiles[slot], preferred_element_type=jnp.float32)
                left_part = left_part + (
                    mixed.reshape(tile // 8, 8, width) * w_wide[k][None]
                ).reshape(tile, width)
                bin_out[k] += (mixed * left_wide).reshape(tile // 8, 8, width).sum(0)
                pieces.append(grad)
                scales.append(left_turn[...] * w_cols[k])
            left_sum[...] += left_part
            right_sum[...] += jnp.dot(
                jnp.concatenate(scales, 1),
                jnp.concatenate(pieces, 0),
                preferred_element_type=jnp.float32,
            )
            return 0

        lax.fori_loop(0, bins // GROUP_GRADS, grads, 0)
        left_grads[slot] = left_sum[...].astype(jnp.bfloat16)
        right_grads[slot] = right_sum[...].T.astype(jnp.bfloat16)
        return 0

    lax.fori_loop(0, live, block, 0)


def run_blocks(place, count, bin_weight, bin_bias, left_from, right_from, teacher):
    slots, bins, tile, _ = teacher.shape
    width = bin_weight.shape[0]
    wide = bin_weight.astype(jnp.float32)
    smem = pl.BlockSpec(memory_space=pltpu.SMEM)
    vmem = pl.BlockSpec(memory_space=pltpu.VMEM)
    hbm = pl.BlockSpec(memory_space=pl.ANY)
    f32, bf16 = jnp.float32, jnp.bfloat16
    piece = jax.ShapeDtypeStruct((slots, tile, width), bf16)
    return pl.pallas_call(
        blocks_kernel,
        out_shape=[piece] * 2
        + [
            jax.ShapeDtypeStruct((bins, 8, width), f32),
            jax.ShapeDtypeStruct((8, tile), f32),
        ],
        in_specs=[smem] * 3 + [vmem] * 2 + [hbm] * 7,
        out_specs=[vmem] * 4,
        scratch_shapes=[
            pltpu.VMEM((bins, 16, width), bf16),
            pltpu.VMEM((bins, 8, width), f32),
            pltpu.VMEM((bins, width, tile), bf16),
            pltpu.VMEM((slots, tile, width), bf16),
            pltpu.VMEM((slots, tile, width), bf16),
            pltpu.VMEM((2, bins, tile, tile), bf16),
            pltpu.VMEM((bins, tile, tile), f32),
            pltpu.VMEM((width, tile), bf16),
            pltpu.VMEM((width, tile), bf16),
            pltpu.VMEM((tile, width), f32),
            pltpu.VMEM((width, tile), f32),
            pltpu.SemaphoreType.DMA((slots, 2)),
            pltpu.SemaphoreType.DMA((2,)),
        ],
        compiler_params=pltpu.CompilerParams(vmem_limit_bytes=48 * 1024 * 1024),
        cost_estimate=pl.CostEstimate(
            flops=6 * 8 * 64 * 128**3, bytes_accessed=20 * 2**20, transcendentals=8 * 2**20
        ),
    )(place, count, bin_bias, wide.T, wide, *left_from, *right_from, teacher)


AXES = ("z", "core", "y", "x")
TILES_DEV = 4


def own_spot(info, s, slot):
    row = info[s, 2 * slot]
    return lax.rem(row // 16, 4), lax.rem(row // 4, 4), lax.rem(row, 4)


def pick_kernel(info, here, near0, near1, near2, near3, out0, out1, out2, out3, bank):
    outs = (out0, out1, out2, out3)
    for n, near in enumerate((near0, near1, near2, near3)):
        bank[pl.ds(4 * n, 4)] = near[...]
    slots = out0.shape[0]
    for s in range(4):
        for slot in range(slots):
            _, x, t = own_spot(info, s, slot)
            spot = lax.rem(here[3] - x + 4, 4) * 4 + t
            outs[(4 - s) % 4][slot] = bank[spot]


def pick_tiles(info, here, near):
    slots = (info.shape[1] - 1) // 2
    _, tile, width = near[0].shape
    smem = pl.BlockSpec(memory_space=pltpu.SMEM)
    vmem = pl.BlockSpec(memory_space=pltpu.VMEM)
    return pl.pallas_call(
        pick_kernel,
        out_shape=[jax.ShapeDtypeStruct((slots, tile, width), near[0].dtype)] * 4,
        in_specs=[smem] * 2 + [vmem] * 4,
        out_specs=[vmem] * 4,
        scratch_shapes=[pltpu.VMEM((16, tile, width), near[0].dtype)],
        compiler_params=pltpu.CompilerParams(vmem_limit_bytes=16 * 1024 * 1024),
    )(info, here, *near)


def fold_kernel(side, info, here, *refs):
    sources, (own, far1, far2, far3, total) = refs[:-5], refs[-5:]
    total[...] = jnp.zeros(total.shape, jnp.float32)
    slots = sources[0].shape[0]
    for s, source in enumerate(sources):
        live = info[s, 2 * slots if side == 0 else 3 * slots]
        for slot in range(slots):
            if side == 0:
                y, x, t = own_spot(info, s, slot)
                mine, spot = y == here[2], lax.rem(x - here[3] + 4, 4) * 4 + t
            else:
                z, core, u = (info[s, n * slots + slot] for n in range(3))
                mine, spot = core == here[1], lax.rem(z - here[0] + 4, 4) * 4 + u

            @pl.when((slot < live) & mine)
            def _():
                total[spot] += source[slot].astype(jnp.float32)

    own[...] = total[pl.ds(0, 4)]
    for n, far in enumerate((far1, far2, far3)):
        far[...] = total[pl.ds(4 * n + 4, 4)].astype(jnp.bfloat16)


def fold_slots(side, info, here, sources):
    _, tile, width = sources[0].shape
    smem = pl.BlockSpec(memory_space=pltpu.SMEM)
    vmem = pl.BlockSpec(memory_space=pltpu.VMEM)
    far = jax.ShapeDtypeStruct((4, tile, width), jnp.bfloat16)
    return pl.pallas_call(
        functools.partial(fold_kernel, side),
        out_shape=[jax.ShapeDtypeStruct((4, tile, width), jnp.float32)] + [far] * 3,
        in_specs=[smem] * 2 + [vmem] * len(sources),
        out_specs=[vmem] * 4,
        scratch_shapes=[pltpu.VMEM((16, tile, width), jnp.float32)],
        compiler_params=pltpu.CompilerParams(vmem_limit_bytes=16 * 1024 * 1024),
    )(info, here, *sources)


def shift(value, axis, step):
    size = lax.axis_size(axis)
    return lax.ppermute(value, axis, [(i, (i + step) % size) for i in range(size)])


def ring(value, axis):
    return [shift(value, axis, s) for s in range(1, lax.axis_size(axis))]


def after(value, *others):
    return lax.optimization_barrier((value,) + others)[0]


def low_parts(value, count):
    parts = []
    for _ in range(count):
        parts.append(value.astype(jnp.bfloat16))
        value = value - parts[-1].astype(jnp.float32)
    return parts


def per_device(
    single, left_weight, right_weight, bin_weight, bin_bias, block_tiles, block_count, teacher
):
    slots, bins, tile = teacher.shape[1:4]
    devices = lax.axis_size(AXES)
    own_tiles = block_tiles[0]
    left_wide = left_weight.astype(jnp.float32)
    right_wide = right_weight.astype(jnp.float32)
    info = jnp.concatenate([own_tiles.reshape(1, -1), block_count[None]], axis=1)
    left_local = jnp.dot(single, left_weight, preferred_element_type=jnp.float32).astype(
        jnp.bfloat16
    )
    rows_dev, width = left_local.shape
    left_local = left_local.reshape(-1, tile, width)
    here = jnp.stack([lax.axis_index(a) for a in AXES]).astype(jnp.int32)
    z, core, y = here[0], here[1], here[2]
    left_near = [left_local] + ring(left_local, "x")
    right_local = jnp.dot(after(single, left_near[1]), right_weight, preferred_element_type=jnp.float32).astype(
        jnp.bfloat16
    )
    right_local = right_local.reshape(-1, tile, width)
    right_ring = ring(right_local, "z")
    info_first = after(info, left_local)
    info_y = jnp.concatenate([info_first] + ring(info_first, "y"))
    picked = pick_tiles(info_y, here, left_near)
    left_from = [picked[0]] + [shift(picked[s], "y", s) for s in (1, 2, 3)]
    row, col = own_tiles[:, 0], own_tiles[:, 1]
    right_ring = after(right_ring, *left_from)
    lists = jnp.concatenate([col // 128 % 4, col // 64 % 2, col % TILES_DEV, block_count])[None]
    packed = jnp.pad(lists.astype(jnp.bfloat16), ((0, 15), (0, width - lists.shape[1])))
    right_near = jnp.concatenate(
        [part.reshape(rows_dev, width) for part in [right_local] + right_ring] + [packed]
    )
    sibling = shift(right_near, "core", 1)
    far_lists = sibling[-16:-15, : lists.shape[1]].astype(jnp.int32)
    info_core = jnp.concatenate([lists, far_lists])
    right_from = [right_near, sibling]
    place = jnp.stack(
        [
            (y - row // 16 % 4) % 4,
            (core - col // 64 % 2) % 2,
            (z - col // 128 % 4) % 4 * TILES_DEV + col % TILES_DEV,
        ],
        axis=1,
    )
    place = after(place, info_core)
    left_slots, right_slots, bins_part, cross_part = run_blocks(
        place, block_count, bin_weight, bin_bias, left_from, right_from, teacher[0]
    )
    left_ring = ring(left_slots, "y")
    right_ring = ring(right_slots, "core")
    right_rows_grad, *right_far = fold_slots(1, info_core, here, [right_slots] + right_ring)
    right_far = [shift(right_far[s - 1], "z", s) for s in (1, 2, 3)]
    left_ring = after(left_ring, *right_far)
    left_rows_grad, *left_far = fold_slots(0, info_y, here, [left_slots] + left_ring)
    for s in (1, 2, 3):
        left_rows_grad = left_rows_grad + shift(left_far[s - 1], "x", s).astype(jnp.float32)
        right_rows_grad = right_rows_grad + right_far[s - 1].astype(jnp.float32)
    left_rows_grad = left_rows_grad.reshape(rows_dev, width)
    right_rows_grad = right_rows_grad.reshape(rows_dev, width)
    single_wide = single.astype(jnp.float32)
    part_left = jnp.dot(single_wide.T, left_rows_grad, precision=lax.Precision.HIGHEST)
    part_right = jnp.dot(single_wide.T, right_rows_grad, precision=lax.Precision.HIGHEST)
    depth = part_left.shape[0]
    rows_sum = 2 * depth + bins
    chunk = rows_sum // devices + 1
    last = rows_sum // chunk, rows_sum % chunk
    bf16, f32 = jnp.bfloat16, jnp.float32
    scalars = jnp.stack(low_parts(jnp.sum(cross_part), 3) + [block_count[0].astype(bf16)])
    packed = jnp.concatenate(
        [
            part_left.astype(bf16),
            part_right.astype(bf16),
            jnp.sum(bins_part, axis=1).astype(bf16),
            jnp.pad(scalars[None], ((0, chunk * devices - rows_sum - 1), (0, width - 4))),
        ]
    ).reshape(devices, chunk, width)
    mine = jnp.sum(lax.all_to_all(packed, AXES, 0, 0).astype(f32), axis=0)
    high, low = low_parts(mine, 2)
    mine = jnp.concatenate([high, low[last[1] : last[1] + 1]])
    totals = lax.all_to_all(
        jnp.broadcast_to(mine[None], (devices, chunk + 1, width)), AXES, 0, 0
    ).astype(f32)
    scalars = totals[last[0], last[1]] + totals[last[0], chunk]
    totals = totals[:, :chunk].reshape(-1, width)
    grad_single = (
        jnp.dot(left_rows_grad, left_wide.T, precision=lax.Precision.HIGHEST)
        + jnp.dot(right_rows_grad, right_wide.T, precision=lax.Precision.HIGHEST)
    ).astype(jnp.bfloat16)
    grad_left = totals[:depth] / devices
    grad_right = totals[depth : 2 * depth] / devices
    grad_bin = totals[2 * depth : rows_sum].T / devices
    cross_total = scalars[0] + scalars[1] + scalars[2]
    loss_value = cross_total / (scalars[3] * (tile * tile))
    return (grad_single, grad_left, grad_right, grad_bin, loss_value)


def solution(mesh):
    torus = Mesh(mesh.devices.reshape(4, 2, 4, 4), AXES)
    return jax.shard_map(
        per_device,
        mesh=torus,
        in_specs=(
            P(AXES, None),
            P(),
            P(),
            P(),
            P(),
            P(AXES, None, None),
            P(AXES),
            P(AXES, None, None, None, None),
        ),
        out_specs=(P(AXES, None), P(), P(), P(), P()),
        check_vma=False,
    )
```

profile of v0, /device:TPU:1, one launch (start us, length us, event | category | flops | bytes accessed | tf_op | source)
XLA Modules:
  0.0 151.2 jit_solution(8989441000148266477)
XLA Ops:
  3.4 2.1 %collective-permute-start = (s32[1,17]{1,0:T(1,128)S(1)}, s32[1,17]{1,0:T(1,128)S(1)}, u32[]{:S(2)}, u32[]{:S(2)}) collective-permute-start(s32[1,17]{1,0:T(1,128)S(1)} %pad_add_fusion.3), channel_id=1, source_target_pairs={{0,4},{4,8},{8,12},{12,0},{1,5},{5,9},{9,13},{13,1},{2,6},{6,10},{... | collective-permute-start | bytes 212 | tf_op jit(solution)/shard_map/ppermute | solution.py:269
  5.6 2.6 %collective-permute-start.1 = (s32[1,17]{1,0:T(1,128)S(1)}, s32[1,17]{1,0:T(1,128)S(1)}, u32[]{:S(2)}, u32[]{:S(2)}) collective-permute-start(s32[1,17]{1,0:T(1,128)S(1)} %pad_add_fusion.3), channel_id=1, source_target_pairs={{0,8},{4,12},{8,0},{12,4},{1,9},{5,13},{9,1},{13,5},{2,10},{6,14},... | collective-permute-start | bytes 212 | tf_op jit(solution)/shard_map/ppermute | solution.py:269
  9.4 2.4 %collective-permute-start.7 = (bf16[4,128,128]{2,1,0:T(8,128)(2,1)S(1)}, bf16[4,128,128]{2,1,0:T(8,128)(2,1)S(1)}, u32[]{:S(2)}, u32[]{:S(2)}) collective-permute-start(bf16[4,128,128]{2,1,0:T(8,128)(2,1)S(1)} %bitcast.76), channel_id=1, source_target_pairs={{0,2},{1,3},{2,0},{3,1},{4,6},{5,7},{6,4},{7,5},{8,10},{9,11},{10,... | collective-permute-start | bytes 393224 | tf_op jit(solution)/shard_map/ppermute | solution.py:269
  14.6 1.8 %constant_dynamic-update-slice_fusion.4 = (bf16[2064,128]{1,0:T(8,128)(2,1)S(1)}, bf16[512,128]{1,0:T(8,128)(2,1)}) fusion(bf16[512,384]{1,0:T(8,128)(2,1)S(1)} %copy-done, bf16[384,128]{1,0:T(8,128)(2,1)} %param.10), kind=kOutput, calls=%fused_computation.23 | convolution fusion | flops 50397184 | bytes 753664 | tf_op jit(solution)/shard_map/dot_general | solution.py:305
  16.4 1.6 %collective-permute-start.4 = (bf16[4,128,128]{2,1,0:T(8,128)(2,1)}, bf16[4,128,128]{2,1,0:T(8,128)(2,1)S(1)}, u32[]{:S(2)}, u32[]{:S(2)}) collective-permute-start(bf16[4,128,128]{2,1,0:T(8,128)(2,1)} %bitcast.8), channel_id=1, source_target_pairs={{0,32},{32,64},{64,96},{96,0},{1,33},{33,65},{65,97},{97,1},{2,34}... | collective-permute-start | bytes 393224 | tf_op jit(solution)/shard_map/ppermute | solution.py:269
  19.2 1.3 collective-permute-done.2
  20.5 3.4 %collective-permute-start.5 = (bf16[4,128,128]{2,1,0:T(8,128)(2,1)}, bf16[4,128,128]{2,1,0:T(8,128)(2,1)S(1)}, u32[]{:S(2)}, u32[]{:S(2)}) collective-permute-start(bf16[4,128,128]{2,1,0:T(8,128)(2,1)} %bitcast.8), channel_id=1, source_target_pairs={{0,64},{32,96},{64,0},{96,32},{1,65},{33,97},{65,1},{97,33},{2,66}... | collective-permute-start | bytes 393224 | tf_op jit(solution)/shard_map/ppermute | solution.py:269
  26.4 1.6 %collective-permute-start.11 = (bf16[8,128,128]{2,1,0:T(8,128)(2,1)S(1)}, bf16[8,128,128]{2,1,0:T(8,128)(2,1)S(1)}, u32[]{:S(2)}, u32[]{:S(2)}) collective-permute-start(bf16[8,128,128]{2,1,0:T(8,128)(2,1)S(1)} %get-tuple-element.35), channel_id=1, source_target_pairs={{0,12},{4,0},{8,4},{12,8},{1,13},{5,1},{9,5},{13,9},{2,14},{6,2},{... | collective-permute-start | bytes 786440 | tf_op jit(solution)/shard_map/ppermute | solution.py:269
  29.6 2.9 %collective-permute-done.10.left2 = bf16[8,128,128]{2,1,0:T(8,128)(2,1)S(1)} collective-permute-done((bf16[8,128,128]{2,1,0:T(8,128)(2,1)S(1)}, bf16[8,128,128]{2,1,0:T(8,128)(2,1)S(1)}, u32[]{:S(2)}, u32[]{:S(2)}) %collective-permute-start.10) | collective-permute-done | bytes 262176 | tf_op jit(solution)/shard_map/ppermute | solution.py:269
  32.4 5.4 %collective-permute-done.11.left3 = bf16[8,128,128]{2,1,0:T(8,128)(2,1)S(1)} collective-permute-done((bf16[8,128,128]{2,1,0:T(8,128)(2,1)S(1)}, bf16[8,128,128]{2,1,0:T(8,128)(2,1)S(1)}, u32[]{:S(2)}, u32[]{:S(2)}) %collective-permute-start.11) | collective-permute-done | bytes 262176 | tf_op jit(solution)/shard_map/ppermute | solution.py:269
  38.0 3.7 %collective-permute-start.12 = (bf16[2064,128]{1,0:T(8,128)(2,1)S(1)}, bf16[2064,128]{1,0:T(8,128)(2,1)S(1)}, u32[]{:S(2)}, u32[]{:S(2)}) collective-permute-start(bf16[2064,128]{1,0:T(8,128)(2,1)S(1)} %constant_dynamic-update-slice_fusion.right0), channel_id=1, source_target_pairs={{0,16},{16,0},{1,17},{17,1},{2,18},{18,2},{3,19},{19,3},{4,20},{20... | collective-permute-start | bytes 1585160 | tf_op jit(solution)/shard_map/ppermute | solution.py:269
  41.8 1.4 collective-permute-done.12.right1
  43.9 14.7 %shard_map.120 = (bf16[8,128,128]{2,1,0:T(8,128)(2,1)S(1)}, bf16[8,128,128]{2,1,0:T(8,128)(2,1)S(1)}, f32[64,8,128]{2,1,0:T(8,128)S(1)}, f32[8,128]{1,0:T(8,128)S(1)}) custom-call(s32[8,3]{1,0:T(8,128)S(1)} %pad_add_fusion.place, s32[1]{0:T(128)} %copy.49.count, f32[64]{0:T(128)S(1)} %copy-done.1, f32[64,128]{1,0:T(8,128)S(1)} %copy.38.w_turned, ...), custom_call_target="tpu_custom_call" | custom-call | flops 6442450944 | bytes 20971520 | tf_op jit(solution)/shard_map/pallas_call | solution.py:162
  58.6 21.8 %collective-permute-start.16 = (bf16[8,128,128]{2,1,0:T(8,128)(2,1)S(1)}, bf16[8,128,128]{2,1,0:T(8,128)(2,1)S(1)}, u32[]{:S(2)}, u32[]{:S(2)}) collective-permute-start(bf16[8,128,128]{2,1,0:T(8,128)(2,1)S(1)} %get-tuple-element.41.refs_0_), channel_id=1, source_target_pairs={{0,16},{16,0},{1,17},{17,1},{2,18},{18,2},{3,19},{19,3},{4,20},{20... | collective-permute-start | bytes 786440 | tf_op jit(solution)/shard_map/ppermute | solution.py:269
  80.4 2.7 %collective-permute-start.15 = (bf16[8,128,128]{2,1,0:T(8,128)(2,1)S(1)}, bf16[8,128,128]{2,1,0:T(8,128)(2,1)S(1)}, u32[]{:S(2)}, u32[]{:S(2)}) collective-permute-start(bf16[8,128,128]{2,1,0:T(8,128)(2,1)S(1)} %get-tuple-element.40.refs_0_), channel_id=1, source_target_pairs={{0,12},{4,0},{8,4},{12,8},{1,13},{5,1},{9,5},{13,9},{2,14},{6,2},{... | collective-permute-start | bytes 786440 | tf_op jit(solution)/shard_map/ppermute | solution.py:269
  84.2 11.1 %collective-permute-done.13.refs_1_ = bf16[8,128,128]{2,1,0:T(8,128)(2,1)S(1)} collective-permute-done((bf16[8,128,128]{2,1,0:T(8,128)(2,1)S(1)}, bf16[8,128,128]{2,1,0:T(8,128)(2,1)S(1)}, u32[]{:S(2)}, u32[]{:S(2)}) %collective-permute-start.13) | collective-permute-done | bytes 262176 | tf_op jit(solution)/shard_map/ppermute | solution.py:269
  97.6 2.0 %collective-permute-done.19 = bf16[4,128,128]{2,1,0:T(8,128)(2,1)S(1)} collective-permute-done((bf16[4,128,128]{2,1,0:T(8,128)(2,1)S(1)}, bf16[4,128,128]{2,1,0:T(8,128)(2,1)S(1)}, u32[]{:S(2)}, u32[]{:S(2)}) %collective-permute-start.19) | collective-permute-done | bytes 131104 | tf_op jit(solution)/shard_map/ppermute | solution.py:269
  99.6 1.5 %shard_map.122 = (f32[4,128,128]{2,1,0:T(8,128)S(1)}, bf16[4,128,128]{2,1,0:T(8,128)(2,1)S(1)}, bf16[4,128,128]{2,1,0:T(8,128)(2,1)S(1)}, bf16[4,128,128]{2,1,0:T(8,128)(2,1)S(1)}) custom-call(s32[4,17]{1,0:T(4,128)S(1)} %pad_add_fusion.1.info, s32[4]{0:T(128)S(1)} %pad_add_fusion.4.here, bf16[8,128,128]{2,1,0:T(8,128)(2,1)S(1)} %get-tuple-element.40.refs_0_, ...), custom_call_target="tpu_custom_call" | custom-call | tf_op jit(solution)/shard_map/pallas_call | solution.py:257
  101.3 2.6 %collective-permute-start.22 = (bf16[4,128,128]{2,1,0:T(8,128)(2,1)S(1)}, bf16[4,128,128]{2,1,0:T(8,128)(2,1)S(1)}, u32[]{:S(2)}, u32[]{:S(2)}) collective-permute-start(bf16[4,128,128]{2,1,0:T(8,128)(2,1)S(1)} %get-tuple-element.51), channel_id=1, source_target_pairs={{0,3},{1,0},{2,1},{3,2},{4,7},{5,4},{6,5},{7,6},{8,11},{9,8},{10,9... | collective-permute-start | bytes 393224 | tf_op jit(solution)/shard_map/ppermute | solution.py:269
  104.4 5.6 %collective-permute-done.20 = bf16[4,128,128]{2,1,0:T(8,128)(2,1)S(1)} collective-permute-done((bf16[4,128,128]{2,1,0:T(8,128)(2,1)S(1)}, bf16[4,128,128]{2,1,0:T(8,128)(2,1)S(1)}, u32[]{:S(2)}, u32[]{:S(2)}) %collective-permute-start.20) | collective-permute-done | bytes 131104 | tf_op jit(solution)/shard_map/ppermute | solution.py:269
  111.6 6.1 %all-to-all-start = ((bf16[128,7,128]{2,1,0:T(8,128)(2,1)}), bf16[128,7,128]{2,1,0:T(8,128)(2,1)S(1)}, u32[]{:S(2)}, u32[]{:S(2)}) async-start(bf16[128,7,128]{2,1,0:T(8,128)(2,1)} %reshape.122), calls=%async_computation | async-start | bytes 524288 | tf_op jit(solution)/shard_map/all_to_all | solution.py:365
  118.2 10.8 %all-to-all-done = bf16[128,7,128]{2,1,0:T(8,128)(2,1)S(1)} async-done(((bf16[128,7,128]{2,1,0:T(8,128)(2,1)}), bf16[128,7,128]{2,1,0:T(8,128)(2,1)S(1)}, u32[]{:S(2)}, u32[]{:S(2)}) %all-to-all-start) | async-done | bytes 229408 | tf_op jit(solution)/shard_map/all_to_all | solution.py:365
  129.9 4.2 %all-to-all-start.1 = ((bf16[128,8,128]{2,1,0:T(8,128)(2,1)}), bf16[128,8,128]{2,1,0:T(8,128)(2,1)S(1)}, u32[]{:S(2)}, u32[]{:S(2)}) async-start(bf16[128,8,128]{2,1,0:T(8,128)(2,1)} %broadcast_in_dim.18), calls=%async_computation.1 | async-start | bytes 524288 | tf_op jit(solution)/shard_map/all_to_all | solution.py:368
  135.4 10.0 %all-to-all-done.1 = bf16[128,8,128]{2,1,0:T(8,128)(2,1)S(1)} async-done(((bf16[128,8,128]{2,1,0:T(8,128)(2,1)}), bf16[128,8,128]{2,1,0:T(8,128)(2,1)S(1)}, u32[]{:S(2)}, u32[]{:S(2)}) %all-to-all-start.1) | async-done | bytes 262176 | tf_op jit(solution)/shard_map/all_to_all | solution.py:368
  (88 shorter events, 21.2 us)
Async XLA Ops:
  3.4 14.7 %collective-permute-start = (s32[1,17]{1,0:T(1,128)S(1)}, s32[1,17]{1,0:T(1,128)S(1)}, u32[]{:S(2)}, u32[]{:S(2)}) collective-permute-start(s32[1,17]{1,0:T(1,128)S(1)} %pad_add_fusion.3), channel_id=1, source_target_pairs={{0,4},{4,8},{8,12},{12,0},{1,5},{5,9},{9,13},{13,1},{2,6},{6,10},{... | collective-permute-start | bytes 212 | tf_op jit(solution)/shard_map/ppermute | solution.py:269
  5.6 13.7 %collective-permute-start.1 = (s32[1,17]{1,0:T(1,128)S(1)}, s32[1,17]{1,0:T(1,128)S(1)}, u32[]{:S(2)}, u32[]{:S(2)}) collective-permute-start(s32[1,17]{1,0:T(1,128)S(1)} %pad_add_fusion.3), channel_id=1, source_target_pairs={{0,8},{4,12},{8,0},{12,4},{1,9},{5,13},{9,1},{13,5},{2,10},{6,14},... | collective-permute-start | bytes 212 | tf_op jit(solution)/shard_map/ppermute | solution.py:269
  8.2 6.4 %collective-permute-start.3 = (bf16[4,128,128]{2,1,0:T(8,128)(2,1)S(1)}, bf16[4,128,128]{2,1,0:T(8,128)(2,1)S(1)}, u32[]{:S(2)}, u32[]{:S(2)}) collective-permute-start(bf16[4,128,128]{2,1,0:T(8,128)(2,1)S(1)} %bitcast.75), channel_id=1, source_target_pairs={{0,1},{1,2},{2,3},{3,0},{4,5},{5,6},{6,7},{7,4},{8,9},{9,10},{10,1... | collective-permute-start | bytes 393224 | tf_op jit(solution)/shard_map/ppermute | solution.py:269
  9.4 15.3 %collective-permute-start.7 = (bf16[4,128,128]{2,1,0:T(8,128)(2,1)S(1)}, bf16[4,128,128]{2,1,0:T(8,128)(2,1)S(1)}, u32[]{:S(2)}, u32[]{:S(2)}) collective-permute-start(bf16[4,128,128]{2,1,0:T(8,128)(2,1)S(1)} %bitcast.76), channel_id=1, source_target_pairs={{0,2},{1,3},{2,0},{3,1},{4,6},{5,7},{6,4},{7,5},{8,10},{9,11},{10,... | collective-permute-start | bytes 393224 | tf_op jit(solution)/shard_map/ppermute | solution.py:269
  11.8 12.8 %collective-permute-start.8 = (bf16[4,128,128]{2,1,0:T(8,128)(2,1)S(1)}, bf16[4,128,128]{2,1,0:T(8,128)(2,1)S(1)}, u32[]{:S(2)}, u32[]{:S(2)}) collective-permute-start(bf16[4,128,128]{2,1,0:T(8,128)(2,1)S(1)} %bitcast.77), channel_id=1, source_target_pairs={{0,3},{1,0},{2,1},{3,2},{4,7},{5,4},{6,5},{7,6},{8,11},{9,8},{10,9... | collective-permute-start | bytes 393224 | tf_op jit(solution)/shard_map/ppermute | solution.py:269
  16.4 11.6 %collective-permute-start.4 = (bf16[4,128,128]{2,1,0:T(8,128)(2,1)}, bf16[4,128,128]{2,1,0:T(8,128)(2,1)S(1)}, u32[]{:S(2)}, u32[]{:S(2)}) collective-permute-start(bf16[4,128,128]{2,1,0:T(8,128)(2,1)} %bitcast.8), channel_id=1, source_target_pairs={{0,32},{32,64},{64,96},{96,0},{1,33},{33,65},{65,97},{97,1},{2,34}... | collective-permute-start | bytes 393224 | tf_op jit(solution)/shard_map/ppermute | solution.py:269
  20.5 9.0 %collective-permute-start.5 = (bf16[4,128,128]{2,1,0:T(8,128)(2,1)}, bf16[4,128,128]{2,1,0:T(8,128)(2,1)S(1)}, u32[]{:S(2)}, u32[]{:S(2)}) collective-permute-start(bf16[4,128,128]{2,1,0:T(8,128)(2,1)} %bitcast.8), channel_id=1, source_target_pairs={{0,64},{32,96},{64,0},{96,32},{1,65},{33,97},{65,1},{97,33},{2,66}... | collective-permute-start | bytes 393224 | tf_op jit(solution)/shard_map/ppermute | solution.py:269
  23.9 5.6 %collective-permute-start.6 = (bf16[4,128,128]{2,1,0:T(8,128)(2,1)}, bf16[4,128,128]{2,1,0:T(8,128)(2,1)S(1)}, u32[]{:S(2)}, u32[]{:S(2)}) collective-permute-start(bf16[4,128,128]{2,1,0:T(8,128)(2,1)} %bitcast.8), channel_id=1, source_target_pairs={{0,96},{32,0},{64,32},{96,64},{1,97},{33,1},{65,33},{97,65},{2,98}... | collective-permute-start | bytes 393224 | tf_op jit(solution)/shard_map/ppermute | solution.py:269
  25.6 6.9 %collective-permute-start.10 = (bf16[8,128,128]{2,1,0:T(8,128)(2,1)S(1)}, bf16[8,128,128]{2,1,0:T(8,128)(2,1)S(1)}, u32[]{:S(2)}, u32[]{:S(2)}) collective-permute-start(bf16[8,128,128]{2,1,0:T(8,128)(2,1)S(1)} %get-tuple-element.34), channel_id=1, source_target_pairs={{0,8},{4,12},{8,0},{12,4},{1,9},{5,13},{9,1},{13,5},{2,10},{6,14},... | collective-permute-start | bytes 786440 | tf_op jit(solution)/shard_map/ppermute | solution.py:269
  26.4 11.4 %collective-permute-start.11 = (bf16[8,128,128]{2,1,0:T(8,128)(2,1)S(1)}, bf16[8,128,128]{2,1,0:T(8,128)(2,1)S(1)}, u32[]{:S(2)}, u32[]{:S(2)}) collective-permute-start(bf16[8,128,128]{2,1,0:T(8,128)(2,1)S(1)} %get-tuple-element.35), channel_id=1, source_target_pairs={{0,12},{4,0},{8,4},{12,8},{1,13},{5,1},{9,5},{13,9},{2,14},{6,2},{... | collective-permute-start | bytes 786440 | tf_op jit(solution)/shard_map/ppermute | solution.py:269
  28.0 9.8 %collective-permute-start.9 = (bf16[8,128,128]{2,1,0:T(8,128)(2,1)S(1)}, bf16[8,128,128]{2,1,0:T(8,128)(2,1)S(1)}, u32[]{:S(2)}, u32[]{:S(2)}) collective-permute-start(bf16[8,128,128]{2,1,0:T(8,128)(2,1)S(1)} %get-tuple-element.33), channel_id=1, source_target_pairs={{0,4},{4,8},{8,12},{12,0},{1,5},{5,9},{9,13},{13,1},{2,6},{6,10},{... | collective-permute-start | bytes 786440 | tf_op jit(solution)/shard_map/ppermute | solution.py:269
  38.0 5.2 %collective-permute-start.12 = (bf16[2064,128]{1,0:T(8,128)(2,1)S(1)}, bf16[2064,128]{1,0:T(8,128)(2,1)S(1)}, u32[]{:S(2)}, u32[]{:S(2)}) collective-permute-start(bf16[2064,128]{1,0:T(8,128)(2,1)S(1)} %constant_dynamic-update-slice_fusion.right0), channel_id=1, source_target_pairs={{0,16},{16,0},{1,17},{17,1},{2,18},{18,2},{3,19},{19,3},{4,20},{20... | collective-permute-start | bytes 1585160 | tf_op jit(solution)/shard_map/ppermute | solution.py:269
  58.6 24.5 %collective-permute-start.16 = (bf16[8,128,128]{2,1,0:T(8,128)(2,1)S(1)}, bf16[8,128,128]{2,1,0:T(8,128)(2,1)S(1)}, u32[]{:S(2)}, u32[]{:S(2)}) collective-permute-start(bf16[8,128,128]{2,1,0:T(8,128)(2,1)S(1)} %get-tuple-element.41.refs_0_), channel_id=1, source_target_pairs={{0,16},{16,0},{1,17},{17,1},{2,18},{18,2},{3,19},{19,3},{4,20},{20... | collective-permute-start | bytes 786440 | tf_op jit(solution)/shard_map/ppermute | solution.py:269
  80.4 14.9 %collective-permute-start.13 = (bf16[8,128,128]{2,1,0:T(8,128)(2,1)S(1)}, bf16[8,128,128]{2,1,0:T(8,128)(2,1)S(1)}, u32[]{:S(2)}, u32[]{:S(2)}) collective-permute-start(bf16[8,128,128]{2,1,0:T(8,128)(2,1)S(1)} %get-tuple-element.40.refs_0_), channel_id=1, source_target_pairs={{0,4},{4,8},{8,12},{12,0},{1,5},{5,9},{9,13},{13,1},{2,6},{6,10},{... | collective-permute-start | bytes 786440 | tf_op jit(solution)/shard_map/ppermute | solution.py:269
  80.4 17.2 %collective-permute-start.14 = (bf16[8,128,128]{2,1,0:T(8,128)(2,1)S(1)}, bf16[8,128,128]{2,1,0:T(8,128)(2,1)S(1)}, u32[]{:S(2)}, u32[]{:S(2)}) collective-permute-start(bf16[8,128,128]{2,1,0:T(8,128)(2,1)S(1)} %get-tuple-element.40.refs_0_), channel_id=1, source_target_pairs={{0,8},{4,12},{8,0},{12,4},{1,9},{5,13},{9,1},{13,5},{2,10},{6,14},... | collective-permute-start | bytes 786440 | tf_op jit(solution)/shard_map/ppermute | solution.py:269
  80.4 17.2 %collective-permute-start.15 = (bf16[8,128,128]{2,1,0:T(8,128)(2,1)S(1)}, bf16[8,128,128]{2,1,0:T(8,128)(2,1)S(1)}, u32[]{:S(2)}, u32[]{:S(2)}) collective-permute-start(bf16[8,128,128]{2,1,0:T(8,128)(2,1)S(1)} %get-tuple-element.40.refs_0_), channel_id=1, source_target_pairs={{0,12},{4,0},{8,4},{12,8},{1,13},{5,1},{9,5},{13,9},{2,14},{6,2},{... | collective-permute-start | bytes 786440 | tf_op jit(solution)/shard_map/ppermute | solution.py:269
  84.0 13.6 %collective-permute-start.17 = (bf16[4,128,128]{2,1,0:T(8,128)(2,1)S(1)}, bf16[4,128,128]{2,1,0:T(8,128)(2,1)S(1)}, u32[]{:S(2)}, u32[]{:S(2)}) collective-permute-start(bf16[4,128,128]{2,1,0:T(8,128)(2,1)S(1)} %get-tuple-element.42), channel_id=1, source_target_pairs={{0,32},{32,64},{64,96},{96,0},{1,33},{33,65},{65,97},{97,1},{2,34}... | collective-permute-start | bytes 393224 | tf_op jit(solution)/shard_map/ppermute | solution.py:269
  84.1 13.5 %collective-permute-start.18 = (bf16[4,128,128]{2,1,0:T(8,128)(2,1)S(1)}, bf16[4,128,128]{2,1,0:T(8,128)(2,1)S(1)}, u32[]{:S(2)}, u32[]{:S(2)}) collective-permute-start(bf16[4,128,128]{2,1,0:T(8,128)(2,1)S(1)} %get-tuple-element.43), channel_id=1, source_target_pairs={{0,64},{32,96},{64,0},{96,32},{1,65},{33,97},{65,1},{97,33},{2,66}... | collective-permute-start | bytes 393224 | tf_op jit(solution)/shard_map/ppermute | solution.py:269
  95.3 4.3 %collective-permute-start.19 = (bf16[4,128,128]{2,1,0:T(8,128)(2,1)S(1)}, bf16[4,128,128]{2,1,0:T(8,128)(2,1)S(1)}, u32[]{:S(2)}, u32[]{:S(2)}) collective-permute-start(bf16[4,128,128]{2,1,0:T(8,128)(2,1)S(1)} %get-tuple-element.44), channel_id=1, source_target_pairs={{0,96},{32,0},{64,32},{96,64},{1,97},{33,1},{65,33},{97,65},{2,98}... | collective-permute-start | bytes 393224 | tf_op jit(solution)/shard_map/ppermute | solution.py:269
  101.1 8.9 %collective-permute-start.20 = (bf16[4,128,128]{2,1,0:T(8,128)(2,1)S(1)}, bf16[4,128,128]{2,1,0:T(8,128)(2,1)S(1)}, u32[]{:S(2)}, u32[]{:S(2)}) collective-permute-start(bf16[4,128,128]{2,1,0:T(8,128)(2,1)S(1)} %get-tuple-element.49), channel_id=1, source_target_pairs={{0,1},{1,2},{2,3},{3,0},{4,5},{5,6},{6,7},{7,4},{8,9},{9,10},{10,1... | collective-permute-start | bytes 393224 | tf_op jit(solution)/shard_map/ppermute | solution.py:269
  101.2 8.8 %collective-permute-start.21 = (bf16[4,128,128]{2,1,0:T(8,128)(2,1)S(1)}, bf16[4,128,128]{2,1,0:T(8,128)(2,1)S(1)}, u32[]{:S(2)}, u32[]{:S(2)}) collective-permute-start(bf16[4,128,128]{2,1,0:T(8,128)(2,1)S(1)} %get-tuple-element.50), channel_id=1, source_target_pairs={{0,2},{1,3},{2,0},{3,1},{4,6},{5,7},{6,4},{7,5},{8,10},{9,11},{10,... | collective-permute-start | bytes 393224 | tf_op jit(solution)/shard_map/ppermute | solution.py:269
  101.3 8.7 %collective-permute-start.22 = (bf16[4,128,128]{2,1,0:T(8,128)(2,1)S(1)}, bf16[4,128,128]{2,1,0:T(8,128)(2,1)S(1)}, u32[]{:S(2)}, u32[]{:S(2)}) collective-permute-start(bf16[4,128,128]{2,1,0:T(8,128)(2,1)S(1)} %get-tuple-element.51), channel_id=1, source_target_pairs={{0,3},{1,0},{2,1},{3,2},{4,7},{5,4},{6,5},{7,6},{8,11},{9,8},{10,9... | collective-permute-start | bytes 393224 | tf_op jit(solution)/shard_map/ppermute | solution.py:269
  111.6 17.4 %all-to-all-start = ((bf16[128,7,128]{2,1,0:T(8,128)(2,1)}), bf16[128,7,128]{2,1,0:T(8,128)(2,1)S(1)}, u32[]{:S(2)}, u32[]{:S(2)}) async-start(bf16[128,7,128]{2,1,0:T(8,128)(2,1)} %reshape.122), calls=%async_computation | async-start | bytes 524288 | tf_op jit(solution)/shard_map/all_to_all | solution.py:365
  129.9 15.5 %all-to-all-start.1 = ((bf16[128,8,128]{2,1,0:T(8,128)(2,1)}), bf16[128,8,128]{2,1,0:T(8,128)(2,1)S(1)}, u32[]{:S(2)}, u32[]{:S(2)}) async-start(bf16[128,8,128]{2,1,0:T(8,128)(2,1)} %broadcast_in_dim.18), calls=%async_computation.1 | async-start | bytes 524288 | tf_op jit(solution)/shard_map/all_to_all | solution.py:368
  (5 other events, 204.8 us)
where the time goes:
time: 151 us
  starting transfers between devices  60.7 us (40%)
  waiting for transfers between devices  50.5 us (33%)
  Pallas kernels  18 us (12%)
  between operations  6.61 us (4%)
  local copies, waits for them, and re-layouts  5.99 us (4%)
  matrix products  5.61 us (4%)
  other arithmetic  3.77 us (2%)
    ppermute x23, starting transfers between devices, shift(): lax.ppermute(value, axis, [(i, (i + step) % size) for i in range(size)])  50.4 us
    ppermute x23, waiting for transfers between devices, shift(): lax.ppermute(value, axis, [(i, (i + step) % size) for i in range(size)])  29.7 us
    pallas_call x1, Pallas kernels, run_blocks(): pl.pallas_call(blocks_kernel, out_shape=[piece] * 2 + [jax.ShapeDtypeStru...  14.7 us
    all_to_all x1, waiting for transfers between devices, per_device(): mine = jnp.sum(lax.all_to_all(packed, AXES, 0, 0).astype(f32), axis=0)  10.8 us
    all_to_all x1, waiting for transfers between devices, per_device(): lax.all_to_all(jnp.broadcast_to(mine[None], (devices, chunk + 1, width)),...  10 us
    all_to_all x1, starting transfers between devices, per_device(): mine = jnp.sum(lax.all_to_all(packed, AXES, 0, 0).astype(f32), axis=0)  6.14 us
    all_to_all x1, starting transfers between devices, per_device(): lax.all_to_all(jnp.broadcast_to(mine[None], (devices, chunk + 1, width)),...  4.2 us
  transfers between devices with their start and end apart: 25, of which 9 were waited for; matrix products, arithmetic and copies ran while one was open for 5% of the time, Pallas kernels for 1%

commit v1 on v0

--- a/solution.py
+++ b/solution.py
@@ -7,9 +7,9 @@
 from jax.sharding import Mesh
 from jax.sharding import PartitionSpec as P
 
-GROUP_SCORES = 32
+GROUP_SCORES = 64
 GROUP_SOFT = 16
-GROUP_GRADS = 32
+GROUP_GRADS = 64
 
 
 def blocks_kernel(
@@ -350,7 +350,7 @@
     part_right = jnp.dot(single_wide.T, right_rows_grad, precision=lax.Precision.HIGHEST)
     depth = part_left.shape[0]
     rows_sum = 2 * depth + bins
-    chunk = rows_sum // devices + 1
+    chunk = 8
     last = rows_sum // chunk, rows_sum % chunk
     bf16, f32 = jnp.bfloat16, jnp.float32
     scalars = jnp.stack(low_parts(jnp.sum(cross_part), 3) + [block_count[0].astype(bf16)])
@@ -364,19 +364,19 @@
     ).reshape(devices, chunk, width)
     mine = jnp.sum(lax.all_to_all(packed, AXES, 0, 0).astype(f32), axis=0)
     high, low = low_parts(mine, 2)
-    mine = jnp.concatenate([high, low[last[1] : last[1] + 1]])
+    here_last = (lax.axis_index(AXES) == last[0]) & (jnp.arange(chunk) == last[1] + 1)
+    mine = jnp.where(here_last[:, None], jnp.roll(low, 1, axis=0), high)
     totals = lax.all_to_all(
-        jnp.broadcast_to(mine[None], (devices, chunk + 1, width)), AXES, 0, 0
-    ).astype(f32)
-    scalars = totals[last[0], last[1]] + totals[last[0], chunk]
-    totals = totals[:, :chunk].reshape(-1, width)
+        jnp.broadcast_to(mine[None], (devices, chunk, width)), AXES, 0, 0
+    ).reshape(-1, width)
+    scalars = jnp.sum(totals[rows_sum : rows_sum + 2].astype(f32), axis=0)
     grad_single = (
         jnp.dot(left_rows_grad, left_wide.T, precision=lax.Precision.HIGHEST)
         + jnp.dot(right_rows_grad, right_wide.T, precision=lax.Precision.HIGHEST)
     ).astype(jnp.bfloat16)
-    grad_left = totals[:depth] / devices
-    grad_right = totals[depth : 2 * depth] / devices
-    grad_bin = totals[2 * depth : rows_sum].T / devices
+    grad_left = totals[:depth].astype(f32) / devices
+    grad_right = totals[depth : 2 * depth].astype(f32) / devices
+    grad_bin = totals[2 * depth : rows_sum].T.astype(f32) / devices
     cross_total = scalars[0] + scalars[1] + scalars[2]
     loss_value = cross_total / (scalars[3] * (tile * tile))
     return (grad_single, grad_left, grad_right, grad_bin, loss_value)

time: 151 us -> 153 us (1.013)
  starting transfers between devices: 60.7 us -> 40.7 us
  Pallas kernels: 18 us -> 37.4 us
  waiting for transfers between devices: 50.5 us -> 52.8 us
    ppermute x23, starting transfers between devices: 50.4 us -> 27.4 us  [shift(): lax.ppermute(value, axis, [(i, (i + step) % size) for i in range(size)])]
    pallas_call x1, Pallas kernels: 14.7 us -> 34.3 us  [run_blocks(): pl.pallas_call(blocks_kernel, out_shape=[piece] * 2 + [jax.ShapeDtypeStru...]
    all_to_all x1, starting transfers between devices: 6.14 us -> 9.05 us  [per_device(): mine = jnp.sum(lax.all_to_all(packed, AXES, 0, 0).astype(f32), axis=0)]
    ppermute x23, waiting for transfers between devices: 29.7 us -> 32 us  [shift(): lax.ppermute(value, axis, [(i, (i + step) % size) for i in range(size)])]
  transfers between devices with their start and end apart: 25 -> 25, of which waited for: 9 -> 12; matrix products, arithmetic and copies ran while one was open for 5% -> 5% of each run, Pallas kernels for 1% -> 1%
where the time goes in v1:
time: 153 us
  waiting for transfers between devices  52.8 us (35%)
  starting transfers between devices  40.7 us (27%)
  Pallas kernels  37.4 us (24%)
  between operations  6.67 us (4%)
  local copies, waits for them, and re-layouts  5.78 us (4%)
  matrix products  5.63 us (4%)
  other arithmetic  3.79 us (2%)
    pallas_call x1, Pallas kernels, run_blocks(): pl.pallas_call(blocks_kernel, out_shape=[piece] * 2 + [jax.ShapeDtypeStru...  34.3 us
    ppermute x23, waiting for transfers between devices, shift(): lax.ppermute(value, axis, [(i, (i + step) % size) for i in range(size)])  32 us
    ppermute x23, starting transfers between devices, shift(): lax.ppermute(value, axis, [(i, (i + step) % size) for i in range(size)])  27.4 us
    all_to_all x1, waiting for transfers between devices, per_device(): mine = jnp.sum(lax.all_to_all(packed, AXES, 0, 0).astype(f32), axis=0)  10.8 us
    all_to_all x1, waiting for transfers between devices, per_device(): lax.all_to_all(jnp.broadcast_to(mine[None], (devices, chunk, width)), AXE...  10 us
    all_to_all x1, starting transfers between devices, per_device(): mine = jnp.sum(lax.all_to_all(packed, AXES, 0, 0).astype(f32), axis=0)  9.05 us
    all_to_all x1, starting transfers between devices, per_device(): lax.all_to_all(jnp.broadcast_to(mine[None], (devices, chunk, width)), AXE...  4.2 us
  transfers between devices with their start and end apart: 25, of which 12 were waited for; matrix products, arithmetic and copies ran while one was open for 5% of the time, Pallas kernels for 1%

profile of v1, /device:TPU:1, one launch (start us, length us, event | category | flops | bytes accessed | tf_op | source)
XLA Modules:
  0.0 152.7 jit_solution(8799081814417407408)
XLA Ops:
  3.5 3.6 %collective-permute-start.2 = (s32[1,17]{1,0:T(1,128)S(1)}, s32[1,17]{1,0:T(1,128)S(1)}, u32[]{:S(2)}, u32[]{:S(2)}) collective-permute-start(s32[1,17]{1,0:T(1,128)S(1)} %pad_add_fusion.3), channel_id=1, source_target_pairs={{0,12},{4,0},{8,4},{12,8},{1,13},{5,1},{9,5},{13,9},{2,14},{6,2},{... | collective-permute-start | bytes 212 | tf_op jit(solution)/shard_map/ppermute | solution.py:269
  7.4 2.5 %collective-permute-start.8 = (bf16[4,128,128]{2,1,0:T(8,128)(2,1)S(1)}, bf16[4,128,128]{2,1,0:T(8,128)(2,1)S(1)}, u32[]{:S(2)}, u32[]{:S(2)}) collective-permute-start(bf16[4,128,128]{2,1,0:T(8,128)(2,1)S(1)} %bitcast.84), channel_id=1, source_target_pairs={{0,3},{1,0},{2,1},{3,2},{4,7},{5,4},{6,5},{7,6},{8,11},{9,8},{10,9... | collective-permute-start | bytes 393224 | tf_op jit(solution)/shard_map/ppermute | solution.py:269
  12.6 6.2 %collective-permute-done.3.near1 = bf16[4,128,128]{2,1,0:T(8,128)(2,1)S(1)} collective-permute-done((bf16[4,128,128]{2,1,0:T(8,128)(2,1)S(1)}, bf16[4,128,128]{2,1,0:T(8,128)(2,1)S(1)}, u32[]{:S(2)}, u32[]{:S(2)}) %collective-permute-start.3) | collective-permute-done | bytes 131104 | tf_op jit(solution)/shard_map/ppermute | solution.py:269
  18.8 1.8 %constant_dynamic-update-slice_fusion.4 = (bf16[2064,128]{1,0:T(8,128)(2,1)S(1)}, bf16[512,128]{1,0:T(8,128)(2,1)}) fusion(bf16[512,384]{1,0:T(8,128)(2,1)S(1)} %copy-done, bf16[384,128]{1,0:T(8,128)(2,1)} %param.10), kind=kOutput, calls=%fused_computation.22 | convolution fusion | flops 50397184 | bytes 753664 | tf_op jit(solution)/shard_map/dot_general | solution.py:305
  20.6 3.8 %collective-permute-start.6 = (bf16[4,128,128]{2,1,0:T(8,128)(2,1)}, bf16[4,128,128]{2,1,0:T(8,128)(2,1)S(1)}, u32[]{:S(2)}, u32[]{:S(2)}) collective-permute-start(bf16[4,128,128]{2,1,0:T(8,128)(2,1)} %bitcast.8), channel_id=1, source_target_pairs={{0,96},{32,0},{64,32},{96,64},{1,97},{33,1},{65,33},{97,65},{2,98}... | collective-permute-start | bytes 393224 | tf_op jit(solution)/shard_map/ppermute | solution.py:269
  25.2 2.9 %collective-permute-done = s32[1,17]{1,0:T(1,128)S(1)} collective-permute-done((s32[1,17]{1,0:T(1,128)S(1)}, s32[1,17]{1,0:T(1,128)S(1)}, u32[]{:S(2)}, u32[]{:S(2)}) %collective-permute-start) | collective-permute-done | bytes 100 | tf_op jit(solution)/shard_map/ppermute | solution.py:269
  29.9 1.5 collective-permute-start.10
  31.4 2.0 %collective-permute-start.11 = (bf16[8,128,128]{2,1,0:T(8,128)(2,1)S(1)}, bf16[8,128,128]{2,1,0:T(8,128)(2,1)S(1)}, u32[]{:S(2)}, u32[]{:S(2)}) collective-permute-start(bf16[8,128,128]{2,1,0:T(8,128)(2,1)S(1)} %get-tuple-element.35), channel_id=1, source_target_pairs={{0,12},{4,0},{8,4},{12,8},{1,13},{5,1},{9,5},{13,9},{2,14},{6,2},{... | collective-permute-start | bytes 786440 | tf_op jit(solution)/shard_map/ppermute | solution.py:269
  34.9 4.6 %collective-permute-done.9.left1 = bf16[8,128,128]{2,1,0:T(8,128)(2,1)S(1)} collective-permute-done((bf16[8,128,128]{2,1,0:T(8,128)(2,1)S(1)}, bf16[8,128,128]{2,1,0:T(8,128)(2,1)S(1)}, u32[]{:S(2)}, u32[]{:S(2)}) %collective-permute-start.9) | collective-permute-done | bytes 262176 | tf_op jit(solution)/shard_map/ppermute | solution.py:269
  39.9 2.8 %collective-permute-done.11.left3 = bf16[8,128,128]{2,1,0:T(8,128)(2,1)S(1)} collective-permute-done((bf16[8,128,128]{2,1,0:T(8,128)(2,1)S(1)}, bf16[8,128,128]{2,1,0:T(8,128)(2,1)S(1)}, u32[]{:S(2)}, u32[]{:S(2)}) %collective-permute-start.11) | collective-permute-done | bytes 262176 | tf_op jit(solution)/shard_map/ppermute | solution.py:269
  42.9 3.4 %collective-permute-start.12 = (bf16[2064,128]{1,0:T(8,128)(2,1)S(1)}, bf16[2064,128]{1,0:T(8,128)(2,1)S(1)}, u32[]{:S(2)}, u32[]{:S(2)}) collective-permute-start(bf16[2064,128]{1,0:T(8,128)(2,1)S(1)} %constant_dynamic-update-slice_fusion.right0), channel_id=1, source_target_pairs={{0,16},{16,0},{1,17},{17,1},{2,18},{18,2},{3,19},{19,3},{4,20},{20... | collective-permute-start | bytes 1585160 | tf_op jit(solution)/shard_map/ppermute | solution.py:269
  46.4 1.4 collective-permute-done.12.right1
  48.5 34.3 %shard_map.120 = (bf16[8,128,128]{2,1,0:T(8,128)(2,1)S(1)}, bf16[8,128,128]{2,1,0:T(8,128)(2,1)S(1)}, f32[64,8,128]{2,1,0:T(8,128)S(1)}, f32[8,128]{1,0:T(8,128)S(1)}) custom-call(s32[8,3]{1,0:T(8,128)S(1)} %pad_add_fusion.place, s32[1]{0:T(128)} %copy.49.count, f32[64]{0:T(128)S(1)} %copy-done.1, f32[64,128]{1,0:T(8,128)S(1)} %copy.38.w_turned, ...), custom_call_target="tpu_custom_call" | custom-call | flops 6442450944 | bytes 20971520 | tf_op jit(solution)/shard_map/pallas_call | solution.py:162
  83.0 2.8 %collective-permute-start.14 = (bf16[8,128,128]{2,1,0:T(8,128)(2,1)S(1)}, bf16[8,128,128]{2,1,0:T(8,128)(2,1)S(1)}, u32[]{:S(2)}, u32[]{:S(2)}) collective-permute-start(bf16[8,128,128]{2,1,0:T(8,128)(2,1)S(1)} %get-tuple-element.40.refs_0_), channel_id=1, source_target_pairs={{0,8},{4,12},{8,0},{12,4},{1,9},{5,13},{9,1},{13,5},{2,10},{6,14},... | collective-permute-start | bytes 786440 | tf_op jit(solution)/shard_map/ppermute | solution.py:269
  86.7 1.4 collective-permute-start.17
  88.1 2.3 %collective-permute-done.15.refs_3_ = bf16[8,128,128]{2,1,0:T(8,128)(2,1)S(1)} collective-permute-done((bf16[8,128,128]{2,1,0:T(8,128)(2,1)S(1)}, bf16[8,128,128]{2,1,0:T(8,128)(2,1)S(1)}, u32[]{:S(2)}, u32[]{:S(2)}) %collective-permute-start.15) | collective-permute-done | bytes 262176 | tf_op jit(solution)/shard_map/ppermute | solution.py:269
  93.2 5.1 %collective-permute-done.13.refs_1_ = bf16[8,128,128]{2,1,0:T(8,128)(2,1)S(1)} collective-permute-done((bf16[8,128,128]{2,1,0:T(8,128)(2,1)S(1)}, bf16[8,128,128]{2,1,0:T(8,128)(2,1)S(1)}, u32[]{:S(2)}, u32[]{:S(2)}) %collective-permute-start.13) | collective-permute-done | bytes 262176 | tf_op jit(solution)/shard_map/ppermute | solution.py:269
  98.4 1.3 shard_map.122
  100.3 2.2 %collective-permute-start.22 = (bf16[4,128,128]{2,1,0:T(8,128)(2,1)S(1)}, bf16[4,128,128]{2,1,0:T(8,128)(2,1)S(1)}, u32[]{:S(2)}, u32[]{:S(2)}) collective-permute-start(bf16[4,128,128]{2,1,0:T(8,128)(2,1)S(1)} %get-tuple-element.51), channel_id=1, source_target_pairs={{0,3},{1,0},{2,1},{3,2},{4,7},{5,4},{6,5},{7,6},{8,11},{9,8},{10,9... | collective-permute-start | bytes 393224 | tf_op jit(solution)/shard_map/ppermute | solution.py:269
  103.0 5.7 %collective-permute-done.20 = bf16[4,128,128]{2,1,0:T(8,128)(2,1)S(1)} collective-permute-done((bf16[4,128,128]{2,1,0:T(8,128)(2,1)S(1)}, bf16[4,128,128]{2,1,0:T(8,128)(2,1)S(1)}, u32[]{:S(2)}, u32[]{:S(2)}) %collective-permute-start.20) | collective-permute-done | bytes 131104 | tf_op jit(solution)/shard_map/ppermute | solution.py:269
  110.2 9.0 %all-to-all-start = ((bf16[128,8,128]{2,1,0:T(8,128)(2,1)}), bf16[128,8,128]{2,1,0:T(8,128)(2,1)S(1)}, u32[]{:S(2)}, u32[]{:S(2)}) async-start(bf16[128,8,128]{2,1,0:T(8,128)(2,1)} %bitcast.25), calls=%async_computation | async-start | bytes 524288 | tf_op jit(solution)/shard_map/all_to_all | solution.py:365
  119.7 10.8 %all-to-all-done = bf16[128,8,128]{2,1,0:T(8,128)(2,1)S(1)} async-done(((bf16[128,8,128]{2,1,0:T(8,128)(2,1)}), bf16[128,8,128]{2,1,0:T(8,128)(2,1)S(1)}, u32[]{:S(2)}, u32[]{:S(2)}) %all-to-all-start) | async-done | bytes 262176 | tf_op jit(solution)/shard_map/all_to_all | solution.py:365
  131.5 4.2 %all-to-all-start.1 = ((bf16[128,8,128]{2,1,0:T(8,128)(2,1)}), bf16[128,8,128]{2,1,0:T(8,128)(2,1)S(1)}, u32[]{:S(2)}, u32[]{:S(2)}) async-start(bf16[128,8,128]{2,1,0:T(8,128)(2,1)} %broadcast_in_dim.28), calls=%async_computation.1 | async-start | bytes 524288 | tf_op jit(solution)/shard_map/all_to_all | solution.py:369
  136.9 10.0 %all-to-all-done.1 = bf16[128,8,128]{2,1,0:T(8,128)(2,1)S(1)} async-done(((bf16[128,8,128]{2,1,0:T(8,128)(2,1)}), bf16[128,8,128]{2,1,0:T(8,128)(2,1)S(1)}, u32[]{:S(2)}, u32[]{:S(2)}) %all-to-all-start.1) | async-done | bytes 262176 | tf_op jit(solution)/shard_map/all_to_all | solution.py:369
  (85 shorter events, 20.3 us)
Async XLA Ops:
  3.5 21.0 %collective-permute-start.2 = (s32[1,17]{1,0:T(1,128)S(1)}, s32[1,17]{1,0:T(1,128)S(1)}, u32[]{:S(2)}, u32[]{:S(2)}) collective-permute-start(s32[1,17]{1,0:T(1,128)S(1)} %pad_add_fusion.3), channel_id=1, source_target_pairs={{0,12},{4,0},{8,4},{12,8},{1,13},{5,1},{9,5},{13,9},{2,14},{6,2},{... | collective-permute-start | bytes 212 | tf_op jit(solution)/shard_map/ppermute | solution.py:269
  7.1 18.1 %collective-permute-start.1 = (s32[1,17]{1,0:T(1,128)S(1)}, s32[1,17]{1,0:T(1,128)S(1)}, u32[]{:S(2)}, u32[]{:S(2)}) collective-permute-start(s32[1,17]{1,0:T(1,128)S(1)} %pad_add_fusion.3), channel_id=1, source_target_pairs={{0,8},{4,12},{8,0},{12,4},{1,9},{5,13},{9,1},{13,5},{2,10},{6,14},... | collective-permute-start | bytes 212 | tf_op jit(solution)/shard_map/ppermute | solution.py:269
  7.4 21.5 %collective-permute-start.8 = (bf16[4,128,128]{2,1,0:T(8,128)(2,1)S(1)}, bf16[4,128,128]{2,1,0:T(8,128)(2,1)S(1)}, u32[]{:S(2)}, u32[]{:S(2)}) collective-permute-start(bf16[4,128,128]{2,1,0:T(8,128)(2,1)S(1)} %bitcast.84), channel_id=1, source_target_pairs={{0,3},{1,0},{2,1},{3,2},{4,7},{5,4},{6,5},{7,6},{8,11},{9,8},{10,9... | collective-permute-start | bytes 393224 | tf_op jit(solution)/shard_map/ppermute | solution.py:269
  9.9 19.0 %collective-permute-start.7 = (bf16[4,128,128]{2,1,0:T(8,128)(2,1)S(1)}, bf16[4,128,128]{2,1,0:T(8,128)(2,1)S(1)}, u32[]{:S(2)}, u32[]{:S(2)}) collective-permute-start(bf16[4,128,128]{2,1,0:T(8,128)(2,1)S(1)} %bitcast.85), channel_id=1, source_target_pairs={{0,2},{1,3},{2,0},{3,1},{4,6},{5,7},{6,4},{7,5},{8,10},{9,11},{10,... | collective-permute-start | bytes 393224 | tf_op jit(solution)/shard_map/ppermute | solution.py:269
  10.4 8.4 %collective-permute-start.3 = (bf16[4,128,128]{2,1,0:T(8,128)(2,1)S(1)}, bf16[4,128,128]{2,1,0:T(8,128)(2,1)S(1)}, u32[]{:S(2)}, u32[]{:S(2)}) collective-permute-start(bf16[4,128,128]{2,1,0:T(8,128)(2,1)S(1)} %bitcast.86), channel_id=1, source_target_pairs={{0,1},{1,2},{2,3},{3,0},{4,5},{5,6},{6,7},{7,4},{8,9},{9,10},{10,1... | collective-permute-start | bytes 393224 | tf_op jit(solution)/shard_map/ppermute | solution.py:269
  20.6 10.7 %collective-permute-start.6 = (bf16[4,128,128]{2,1,0:T(8,128)(2,1)}, bf16[4,128,128]{2,1,0:T(8,128)(2,1)S(1)}, u32[]{:S(2)}, u32[]{:S(2)}) collective-permute-start(bf16[4,128,128]{2,1,0:T(8,128)(2,1)} %bitcast.8), channel_id=1, source_target_pairs={{0,96},{32,0},{64,32},{96,64},{1,97},{33,1},{65,33},{97,65},{2,98}... | collective-permute-start | bytes 393224 | tf_op jit(solution)/shard_map/ppermute | solution.py:269
  24.5 3.6 %collective-permute-start = (s32[1,17]{1,0:T(1,128)S(1)}, s32[1,17]{1,0:T(1,128)S(1)}, u32[]{:S(2)}, u32[]{:S(2)}) collective-permute-start(s32[1,17]{1,0:T(1,128)S(1)} %pad_add_fusion.3), channel_id=1, source_target_pairs={{0,4},{4,8},{8,12},{12,0},{1,5},{5,9},{9,13},{13,1},{2,6},{6,10},{... | collective-permute-start | bytes 212 | tf_op jit(solution)/shard_map/ppermute | solution.py:269
  28.1 6.3 %collective-permute-start.5 = (bf16[4,128,128]{2,1,0:T(8,128)(2,1)}, bf16[4,128,128]{2,1,0:T(8,128)(2,1)S(1)}, u32[]{:S(2)}, u32[]{:S(2)}) collective-permute-start(bf16[4,128,128]{2,1,0:T(8,128)(2,1)} %bitcast.8), channel_id=1, source_target_pairs={{0,64},{32,96},{64,0},{96,32},{1,65},{33,97},{65,1},{97,33},{2,66}... | collective-permute-start | bytes 393224 | tf_op jit(solution)/shard_map/ppermute | solution.py:269
  28.2 6.7 %collective-permute-start.4 = (bf16[4,128,128]{2,1,0:T(8,128)(2,1)}, bf16[4,128,128]{2,1,0:T(8,128)(2,1)S(1)}, u32[]{:S(2)}, u32[]{:S(2)}) collective-permute-start(bf16[4,128,128]{2,1,0:T(8,128)(2,1)} %bitcast.8), channel_id=1, source_target_pairs={{0,32},{32,64},{64,96},{96,0},{1,33},{33,65},{65,97},{97,1},{2,34}... | collective-permute-start | bytes 393224 | tf_op jit(solution)/shard_map/ppermute | solution.py:269
  29.8 9.7 %collective-permute-start.9 = (bf16[8,128,128]{2,1,0:T(8,128)(2,1)S(1)}, bf16[8,128,128]{2,1,0:T(8,128)(2,1)S(1)}, u32[]{:S(2)}, u32[]{:S(2)}) collective-permute-start(bf16[8,128,128]{2,1,0:T(8,128)(2,1)S(1)} %get-tuple-element.33), channel_id=1, source_target_pairs={{0,4},{4,8},{8,12},{12,0},{1,5},{5,9},{9,13},{13,1},{2,6},{6,10},{... | collective-permute-start | bytes 786440 | tf_op jit(solution)/shard_map/ppermute | solution.py:269
  29.9 10.0 %collective-permute-start.10 = (bf16[8,128,128]{2,1,0:T(8,128)(2,1)S(1)}, bf16[8,128,128]{2,1,0:T(8,128)(2,1)S(1)}, u32[]{:S(2)}, u32[]{:S(2)}) collective-permute-start(bf16[8,128,128]{2,1,0:T(8,128)(2,1)S(1)} %get-tuple-element.34), channel_id=1, source_target_pairs={{0,8},{4,12},{8,0},{12,4},{1,9},{5,13},{9,1},{13,5},{2,10},{6,14},... | collective-permute-start | bytes 786440 | tf_op jit(solution)/shard_map/ppermute | solution.py:269
  31.4 11.3 %collective-permute-start.11 = (bf16[8,128,128]{2,1,0:T(8,128)(2,1)S(1)}, bf16[8,128,128]{2,1,0:T(8,128)(2,1)S(1)}, u32[]{:S(2)}, u32[]{:S(2)}) collective-permute-start(bf16[8,128,128]{2,1,0:T(8,128)(2,1)S(1)} %get-tuple-element.35), channel_id=1, source_target_pairs={{0,12},{4,0},{8,4},{12,8},{1,13},{5,1},{9,5},{13,9},{2,14},{6,2},{... | collective-permute-start | bytes 786440 | tf_op jit(solution)/shard_map/ppermute | solution.py:269
  42.9 4.9 %collective-permute-start.12 = (bf16[2064,128]{1,0:T(8,128)(2,1)S(1)}, bf16[2064,128]{1,0:T(8,128)(2,1)S(1)}, u32[]{:S(2)}, u32[]{:S(2)}) collective-permute-start(bf16[2064,128]{1,0:T(8,128)(2,1)S(1)} %constant_dynamic-update-slice_fusion.right0), channel_id=1, source_target_pairs={{0,16},{16,0},{1,17},{17,1},{2,18},{18,2},{3,19},{19,3},{4,20},{20... | collective-permute-start | bytes 1585160 | tf_op jit(solution)/shard_map/ppermute | solution.py:269
  82.9 7.5 %collective-permute-start.15 = (bf16[8,128,128]{2,1,0:T(8,128)(2,1)S(1)}, bf16[8,128,128]{2,1,0:T(8,128)(2,1)S(1)}, u32[]{:S(2)}, u32[]{:S(2)}) collective-permute-start(bf16[8,128,128]{2,1,0:T(8,128)(2,1)S(1)} %get-tuple-element.40.refs_0_), channel_id=1, source_target_pairs={{0,12},{4,0},{8,4},{12,8},{1,13},{5,1},{9,5},{13,9},{2,14},{6,2},{... | collective-permute-start | bytes 786440 | tf_op jit(solution)/shard_map/ppermute | solution.py:269
  83.0 10.3 %collective-permute-start.14 = (bf16[8,128,128]{2,1,0:T(8,128)(2,1)S(1)}, bf16[8,128,128]{2,1,0:T(8,128)(2,1)S(1)}, u32[]{:S(2)}, u32[]{:S(2)}) collective-permute-start(bf16[8,128,128]{2,1,0:T(8,128)(2,1)S(1)} %get-tuple-element.40.refs_0_), channel_id=1, source_target_pairs={{0,8},{4,12},{8,0},{12,4},{1,9},{5,13},{9,1},{13,5},{2,10},{6,14},... | collective-permute-start | bytes 786440 | tf_op jit(solution)/shard_map/ppermute | solution.py:269
  85.8 12.6 %collective-permute-start.13 = (bf16[8,128,128]{2,1,0:T(8,128)(2,1)S(1)}, bf16[8,128,128]{2,1,0:T(8,128)(2,1)S(1)}, u32[]{:S(2)}, u32[]{:S(2)}) collective-permute-start(bf16[8,128,128]{2,1,0:T(8,128)(2,1)S(1)} %get-tuple-element.40.refs_0_), channel_id=1, source_target_pairs={{0,4},{4,8},{8,12},{12,0},{1,5},{5,9},{9,13},{13,1},{2,6},{6,10},{... | collective-permute-start | bytes 786440 | tf_op jit(solution)/shard_map/ppermute | solution.py:269
  86.7 11.7 %collective-permute-start.17 = (bf16[4,128,128]{2,1,0:T(8,128)(2,1)S(1)}, bf16[4,128,128]{2,1,0:T(8,128)(2,1)S(1)}, u32[]{:S(2)}, u32[]{:S(2)}) collective-permute-start(bf16[4,128,128]{2,1,0:T(8,128)(2,1)S(1)} %get-tuple-element.42), channel_id=1, source_target_pairs={{0,32},{32,64},{64,96},{96,0},{1,33},{33,65},{65,97},{97,1},{2,34}... | collective-permute-start | bytes 393224 | tf_op jit(solution)/shard_map/ppermute | solution.py:269
  88.0 10.3 %collective-permute-start.18 = (bf16[4,128,128]{2,1,0:T(8,128)(2,1)S(1)}, bf16[4,128,128]{2,1,0:T(8,128)(2,1)S(1)}, u32[]{:S(2)}, u32[]{:S(2)}) collective-permute-start(bf16[4,128,128]{2,1,0:T(8,128)(2,1)S(1)} %get-tuple-element.43), channel_id=1, source_target_pairs={{0,64},{32,96},{64,0},{96,32},{1,65},{33,97},{65,1},{97,33},{2,66}... | collective-permute-start | bytes 393224 | tf_op jit(solution)/shard_map/ppermute | solution.py:269
  90.4 8.0 %collective-permute-start.19 = (bf16[4,128,128]{2,1,0:T(8,128)(2,1)S(1)}, bf16[4,128,128]{2,1,0:T(8,128)(2,1)S(1)}, u32[]{:S(2)}, u32[]{:S(2)}) collective-permute-start(bf16[4,128,128]{2,1,0:T(8,128)(2,1)S(1)} %get-tuple-element.44), channel_id=1, source_target_pairs={{0,96},{32,0},{64,32},{96,64},{1,97},{33,1},{65,33},{97,65},{2,98}... | collective-permute-start | bytes 393224 | tf_op jit(solution)/shard_map/ppermute | solution.py:269
  99.7 9.0 %collective-permute-start.20 = (bf16[4,128,128]{2,1,0:T(8,128)(2,1)S(1)}, bf16[4,128,128]{2,1,0:T(8,128)(2,1)S(1)}, u32[]{:S(2)}, u32[]{:S(2)}) collective-permute-start(bf16[4,128,128]{2,1,0:T(8,128)(2,1)S(1)} %get-tuple-element.49), channel_id=1, source_target_pairs={{0,1},{1,2},{2,3},{3,0},{4,5},{5,6},{6,7},{7,4},{8,9},{9,10},{10,1... | collective-permute-start | bytes 393224 | tf_op jit(solution)/shard_map/ppermute | solution.py:269
  99.8 8.9 %collective-permute-start.21 = (bf16[4,128,128]{2,1,0:T(8,128)(2,1)S(1)}, bf16[4,128,128]{2,1,0:T(8,128)(2,1)S(1)}, u32[]{:S(2)}, u32[]{:S(2)}) collective-permute-start(bf16[4,128,128]{2,1,0:T(8,128)(2,1)S(1)} %get-tuple-element.50), channel_id=1, source_target_pairs={{0,2},{1,3},{2,0},{3,1},{4,6},{5,7},{6,4},{7,5},{8,10},{9,11},{10,... | collective-permute-start | bytes 393224 | tf_op jit(solution)/shard_map/ppermute | solution.py:269
  100.3 8.4 %collective-permute-start.22 = (bf16[4,128,128]{2,1,0:T(8,128)(2,1)S(1)}, bf16[4,128,128]{2,1,0:T(8,128)(2,1)S(1)}, u32[]{:S(2)}, u32[]{:S(2)}) collective-permute-start(bf16[4,128,128]{2,1,0:T(8,128)(2,1)S(1)} %get-tuple-element.51), channel_id=1, source_target_pairs={{0,3},{1,0},{2,1},{3,2},{4,7},{5,4},{6,5},{7,6},{8,11},{9,8},{10,9... | collective-permute-start | bytes 393224 | tf_op jit(solution)/shard_map/ppermute | solution.py:269
  110.2 20.3 %all-to-all-start = ((bf16[128,8,128]{2,1,0:T(8,128)(2,1)}), bf16[128,8,128]{2,1,0:T(8,128)(2,1)S(1)}, u32[]{:S(2)}, u32[]{:S(2)}) async-start(bf16[128,8,128]{2,1,0:T(8,128)(2,1)} %bitcast.25), calls=%async_computation | async-start | bytes 524288 | tf_op jit(solution)/shard_map/all_to_all | solution.py:365
  131.5 15.5 %all-to-all-start.1 = ((bf16[128,8,128]{2,1,0:T(8,128)(2,1)}), bf16[128,8,128]{2,1,0:T(8,128)(2,1)S(1)}, u32[]{:S(2)}, u32[]{:S(2)}) async-start(bf16[128,8,128]{2,1,0:T(8,128)(2,1)} %broadcast_in_dim.28), calls=%async_computation.1 | async-start | bytes 524288 | tf_op jit(solution)/shard_map/all_to_all | solution.py:369
  (5 other events, 215.2 us)

commit v2 on v0

--- a/solution.py
+++ b/solution.py
@@ -7,9 +7,9 @@
 from jax.sharding import Mesh
 from jax.sharding import PartitionSpec as P
 
-GROUP_SCORES = 32
+GROUP_SCORES = 64
 GROUP_SOFT = 16
-GROUP_GRADS = 32
+GROUP_GRADS = 64
 
 
 def blocks_kernel(

time: 151 us -> 146 us (0.967)
  waiting for transfers between devices: 50.5 us -> 38.2 us
  starting transfers between devices: 60.7 us -> 72.5 us
  Pallas kernels: 18 us -> 13 us
    ppermute x23, waiting for transfers between devices: 29.7 us -> 17.4 us  [shift(): lax.ppermute(value, axis, [(i, (i + step) % size) for i in range(size)])]
    ppermute x23, starting transfers between devices: 50.4 us -> 58.6 us  [shift(): lax.ppermute(value, axis, [(i, (i + step) % size) for i in range(size)])]
    pallas_call x1, Pallas kernels: 14.7 us -> 9.99 us  [run_blocks(): pl.pallas_call(blocks_kernel, out_shape=[piece] * 2 + [jax.ShapeDtypeStru...]
    all_to_all x1, starting transfers between devices: 6.14 us -> 9.71 us  [per_device(): mine = jnp.sum(lax.all_to_all(packed, AXES, 0, 0).astype(f32), axis=0)]
  transfers between devices with their start and end apart: 25 -> 25, of which waited for: 9 -> 10; matrix products, arithmetic and copies ran while one was open for 5% -> 5% of each run, Pallas kernels for 1% -> 1%
where the time goes in v2:
time: 146 us
  starting transfers between devices  72.5 us (50%)
  waiting for transfers between devices  38.2 us (26%)
  Pallas kernels  13 us (9%)
  between operations  6.56 us (4%)
  local copies, waits for them, and re-layouts  5.99 us (4%)
  matrix products  5.61 us (4%)
  other arithmetic  3.77 us (3%)
    ppermute x23, starting transfers between devices, shift(): lax.ppermute(value, axis, [(i, (i + step) % size) for i in range(size)])  58.6 us
    ppermute x23, waiting for transfers between devices, shift(): lax.ppermute(value, axis, [(i, (i + step) % size) for i in range(size)])  17.4 us
    all_to_all x1, waiting for transfers between devices, per_device(): mine = jnp.sum(lax.all_to_all(packed, AXES, 0, 0).astype(f32), axis=0)  10.8 us
    all_to_all x1, waiting for transfers between devices, per_device(): lax.all_to_all(jnp.broadcast_to(mine[None], (devices, chunk + 1, width)),...  10 us
    pallas_call x1, Pallas kernels, run_blocks(): pl.pallas_call(blocks_kernel, out_shape=[piece] * 2 + [jax.ShapeDtypeStru...  9.99 us
    all_to_all x1, starting transfers between devices, per_device(): mine = jnp.sum(lax.all_to_all(packed, AXES, 0, 0).astype(f32), axis=0)  9.71 us
    all_to_all x1, starting transfers between devices, per_device(): lax.all_to_all(jnp.broadcast_to(mine[None], (devices, chunk + 1, width)),...  4.2 us
  transfers between devices with their start and end apart: 25, of which 10 were waited for; matrix products, arithmetic and copies ran while one was open for 5% of the time, Pallas kernels for 1%

profile of v2, /device:TPU:1, one launch (start us, length us, event | category | flops | bytes accessed | tf_op | source)
XLA Modules:
  0.0 145.6 jit_solution(16397388302118105263)
XLA Ops:
  3.4 2.1 %collective-permute-start = (s32[1,17]{1,0:T(1,128)S(1)}, s32[1,17]{1,0:T(1,128)S(1)}, u32[]{:S(2)}, u32[]{:S(2)}) collective-permute-start(s32[1,17]{1,0:T(1,128)S(1)} %pad_add_fusion.3), channel_id=1, source_target_pairs={{0,4},{4,8},{8,12},{12,0},{1,5},{5,9},{9,13},{13,1},{2,6},{6,10},{... | collective-permute-start | bytes 212 | tf_op jit(solution)/shard_map/ppermute | solution.py:269
  5.6 2.6 %collective-permute-start.1 = (s32[1,17]{1,0:T(1,128)S(1)}, s32[1,17]{1,0:T(1,128)S(1)}, u32[]{:S(2)}, u32[]{:S(2)}) collective-permute-start(s32[1,17]{1,0:T(1,128)S(1)} %pad_add_fusion.3), channel_id=1, source_target_pairs={{0,8},{4,12},{8,0},{12,4},{1,9},{5,13},{9,1},{13,5},{2,10},{6,14},... | collective-permute-start | bytes 212 | tf_op jit(solution)/shard_map/ppermute | solution.py:269
  9.4 2.4 %collective-permute-start.7 = (bf16[4,128,128]{2,1,0:T(8,128)(2,1)S(1)}, bf16[4,128,128]{2,1,0:T(8,128)(2,1)S(1)}, u32[]{:S(2)}, u32[]{:S(2)}) collective-permute-start(bf16[4,128,128]{2,1,0:T(8,128)(2,1)S(1)} %bitcast.76), channel_id=1, source_target_pairs={{0,2},{1,3},{2,0},{3,1},{4,6},{5,7},{6,4},{7,5},{8,10},{9,11},{10,... | collective-permute-start | bytes 393224 | tf_op jit(solution)/shard_map/ppermute | solution.py:269
  14.6 1.8 %constant_dynamic-update-slice_fusion.4 = (bf16[2064,128]{1,0:T(8,128)(2,1)S(1)}, bf16[512,128]{1,0:T(8,128)(2,1)}) fusion(bf16[512,384]{1,0:T(8,128)(2,1)S(1)} %copy-done, bf16[384,128]{1,0:T(8,128)(2,1)} %param.10), kind=kOutput, calls=%fused_computation.23 | convolution fusion | flops 50397184 | bytes 753664 | tf_op jit(solution)/shard_map/dot_general | solution.py:305
  16.4 1.6 %collective-permute-start.4 = (bf16[4,128,128]{2,1,0:T(8,128)(2,1)}, bf16[4,128,128]{2,1,0:T(8,128)(2,1)S(1)}, u32[]{:S(2)}, u32[]{:S(2)}) collective-permute-start(bf16[4,128,128]{2,1,0:T(8,128)(2,1)} %bitcast.8), channel_id=1, source_target_pairs={{0,32},{32,64},{64,96},{96,0},{1,33},{33,65},{65,97},{97,1},{2,34}... | collective-permute-start | bytes 393224 | tf_op jit(solution)/shard_map/ppermute | solution.py:269
  20.5 3.4 %collective-permute-start.5 = (bf16[4,128,128]{2,1,0:T(8,128)(2,1)}, bf16[4,128,128]{2,1,0:T(8,128)(2,1)S(1)}, u32[]{:S(2)}, u32[]{:S(2)}) collective-permute-start(bf16[4,128,128]{2,1,0:T(8,128)(2,1)} %bitcast.8), channel_id=1, source_target_pairs={{0,64},{32,96},{64,0},{96,32},{1,65},{33,97},{65,1},{97,33},{2,66}... | collective-permute-start | bytes 393224 | tf_op jit(solution)/shard_map/ppermute | solution.py:269
  26.4 1.6 %collective-permute-start.11 = (bf16[8,128,128]{2,1,0:T(8,128)(2,1)S(1)}, bf16[8,128,128]{2,1,0:T(8,128)(2,1)S(1)}, u32[]{:S(2)}, u32[]{:S(2)}) collective-permute-start(bf16[8,128,128]{2,1,0:T(8,128)(2,1)S(1)} %get-tuple-element.35), channel_id=1, source_target_pairs={{0,12},{4,0},{8,4},{12,8},{1,13},{5,1},{9,5},{13,9},{2,14},{6,2},{... | collective-permute-start | bytes 786440 | tf_op jit(solution)/shard_map/ppermute | solution.py:269
  29.6 2.9 %collective-permute-done.10.left2 = bf16[8,128,128]{2,1,0:T(8,128)(2,1)S(1)} collective-permute-done((bf16[8,128,128]{2,1,0:T(8,128)(2,1)S(1)}, bf16[8,128,128]{2,1,0:T(8,128)(2,1)S(1)}, u32[]{:S(2)}, u32[]{:S(2)}) %collective-permute-start.10) | collective-permute-done | bytes 262176 | tf_op jit(solution)/shard_map/ppermute | solution.py:269
  32.4 5.4 %collective-permute-done.11.left3 = bf16[8,128,128]{2,1,0:T(8,128)(2,1)S(1)} collective-permute-done((bf16[8,128,128]{2,1,0:T(8,128)(2,1)S(1)}, bf16[8,128,128]{2,1,0:T(8,128)(2,1)S(1)}, u32[]{:S(2)}, u32[]{:S(2)}) %collective-permute-start.11) | collective-permute-done | bytes 262176 | tf_op jit(solution)/shard_map/ppermute | solution.py:269
  38.0 3.7 %collective-permute-start.12 = (bf16[2064,128]{1,0:T(8,128)(2,1)S(1)}, bf16[2064,128]{1,0:T(8,128)(2,1)S(1)}, u32[]{:S(2)}, u32[]{:S(2)}) collective-permute-start(bf16[2064,128]{1,0:T(8,128)(2,1)S(1)} %constant_dynamic-update-slice_fusion.right0), channel_id=1, source_target_pairs={{0,16},{16,0},{1,17},{17,1},{2,18},{18,2},{3,19},{19,3},{4,20},{20... | collective-permute-start | bytes 1585160 | tf_op jit(solution)/shard_map/ppermute | solution.py:269
  41.8 1.4 collective-permute-done.12.right1
  43.9 10.0 %shard_map.120 = (bf16[8,128,128]{2,1,0:T(8,128)(2,1)S(1)}, bf16[8,128,128]{2,1,0:T(8,128)(2,1)S(1)}, f32[64,8,128]{2,1,0:T(8,128)S(1)}, f32[8,128]{1,0:T(8,128)S(1)}) custom-call(s32[8,3]{1,0:T(8,128)S(1)} %pad_add_fusion.place, s32[1]{0:T(128)} %copy.49.count, f32[64]{0:T(128)S(1)} %copy-done.1, f32[64,128]{1,0:T(8,128)S(1)} %copy.38.w_turned, ...), custom_call_target="tpu_custom_call" | custom-call | flops 6442450944 | bytes 20971520 | tf_op jit(solution)/shard_map/pallas_call | solution.py:162
  53.9 4.5 %collective-permute-start.16 = (bf16[8,128,128]{2,1,0:T(8,128)(2,1)S(1)}, bf16[8,128,128]{2,1,0:T(8,128)(2,1)S(1)}, u32[]{:S(2)}, u32[]{:S(2)}) collective-permute-start(bf16[8,128,128]{2,1,0:T(8,128)(2,1)S(1)} %get-tuple-element.41.refs_0_), channel_id=1, source_target_pairs={{0,16},{16,0},{1,17},{17,1},{2,18},{18,2},{3,19},{19,3},{4,20},{20... | collective-permute-start | bytes 786440 | tf_op jit(solution)/shard_map/ppermute | solution.py:269
  58.4 17.0 %collective-permute-start.14 = (bf16[8,128,128]{2,1,0:T(8,128)(2,1)S(1)}, bf16[8,128,128]{2,1,0:T(8,128)(2,1)S(1)}, u32[]{:S(2)}, u32[]{:S(2)}) collective-permute-start(bf16[8,128,128]{2,1,0:T(8,128)(2,1)S(1)} %get-tuple-element.40.refs_0_), channel_id=1, source_target_pairs={{0,8},{4,12},{8,0},{12,4},{1,9},{5,13},{9,1},{13,5},{2,10},{6,14},... | collective-permute-start | bytes 786440 | tf_op jit(solution)/shard_map/ppermute | solution.py:269
  75.4 2.1 %collective-permute-start.15 = (bf16[8,128,128]{2,1,0:T(8,128)(2,1)S(1)}, bf16[8,128,128]{2,1,0:T(8,128)(2,1)S(1)}, u32[]{:S(2)}, u32[]{:S(2)}) collective-permute-start(bf16[8,128,128]{2,1,0:T(8,128)(2,1)S(1)} %get-tuple-element.40.refs_0_), channel_id=1, source_target_pairs={{0,12},{4,0},{8,4},{12,8},{1,13},{5,1},{9,5},{13,9},{2,14},{6,2},{... | collective-permute-start | bytes 786440 | tf_op jit(solution)/shard_map/ppermute | solution.py:269
  79.5 2.7 %collective-permute-start.19 = (bf16[4,128,128]{2,1,0:T(8,128)(2,1)S(1)}, bf16[4,128,128]{2,1,0:T(8,128)(2,1)S(1)}, u32[]{:S(2)}, u32[]{:S(2)}) collective-permute-start(bf16[4,128,128]{2,1,0:T(8,128)(2,1)S(1)} %get-tuple-element.44), channel_id=1, source_target_pairs={{0,96},{32,0},{64,32},{96,64},{1,97},{33,1},{65,33},{97,65},{2,98}... | collective-permute-start | bytes 393224 | tf_op jit(solution)/shard_map/ppermute | solution.py:269
  84.5 3.0 %collective-permute-done.14.refs_2_ = bf16[8,128,128]{2,1,0:T(8,128)(2,1)S(1)} collective-permute-done((bf16[8,128,128]{2,1,0:T(8,128)(2,1)S(1)}, bf16[8,128,128]{2,1,0:T(8,128)(2,1)S(1)}, u32[]{:S(2)}, u32[]{:S(2)}) %collective-permute-start.14) | collective-permute-done | bytes 262176 | tf_op jit(solution)/shard_map/ppermute | solution.py:269
  89.3 5.6 %collective-permute-start.20 = (bf16[4,128,128]{2,1,0:T(8,128)(2,1)S(1)}, bf16[4,128,128]{2,1,0:T(8,128)(2,1)S(1)}, u32[]{:S(2)}, u32[]{:S(2)}) collective-permute-start(bf16[4,128,128]{2,1,0:T(8,128)(2,1)S(1)} %get-tuple-element.49), channel_id=1, source_target_pairs={{0,1},{1,2},{2,3},{3,0},{4,5},{5,6},{6,7},{7,4},{8,9},{9,10},{10,1... | collective-permute-start | bytes 393224 | tf_op jit(solution)/shard_map/ppermute | solution.py:269
  95.4 2.1 %collective-permute-start.22 = (bf16[4,128,128]{2,1,0:T(8,128)(2,1)S(1)}, bf16[4,128,128]{2,1,0:T(8,128)(2,1)S(1)}, u32[]{:S(2)}, u32[]{:S(2)}) collective-permute-start(bf16[4,128,128]{2,1,0:T(8,128)(2,1)S(1)} %get-tuple-element.51), channel_id=1, source_target_pairs={{0,3},{1,0},{2,1},{3,2},{4,7},{5,4},{6,5},{7,6},{8,11},{9,8},{10,9... | collective-permute-start | bytes 393224 | tf_op jit(solution)/shard_map/ppermute | solution.py:269
  98.0 2.5 %collective-permute-done.21 = bf16[4,128,128]{2,1,0:T(8,128)(2,1)S(1)} collective-permute-done((bf16[4,128,128]{2,1,0:T(8,128)(2,1)S(1)}, bf16[4,128,128]{2,1,0:T(8,128)(2,1)S(1)}, u32[]{:S(2)}, u32[]{:S(2)}) %collective-permute-start.21) | collective-permute-done | bytes 131104 | tf_op jit(solution)/shard_map/ppermute | solution.py:269
  102.5 9.7 %all-to-all-start = ((bf16[128,7,128]{2,1,0:T(8,128)(2,1)}), bf16[128,7,128]{2,1,0:T(8,128)(2,1)S(1)}, u32[]{:S(2)}, u32[]{:S(2)}) async-start(bf16[128,7,128]{2,1,0:T(8,128)(2,1)} %reshape.122), calls=%async_computation | async-start | bytes 524288 | tf_op jit(solution)/shard_map/all_to_all | solution.py:365
  112.7 10.8 %all-to-all-done = bf16[128,7,128]{2,1,0:T(8,128)(2,1)S(1)} async-done(((bf16[128,7,128]{2,1,0:T(8,128)(2,1)}), bf16[128,7,128]{2,1,0:T(8,128)(2,1)S(1)}, u32[]{:S(2)}, u32[]{:S(2)}) %all-to-all-start) | async-done | bytes 229408 | tf_op jit(solution)/shard_map/all_to_all | solution.py:365
  124.3 4.2 %all-to-all-start.1 = ((bf16[128,8,128]{2,1,0:T(8,128)(2,1)}), bf16[128,8,128]{2,1,0:T(8,128)(2,1)S(1)}, u32[]{:S(2)}, u32[]{:S(2)}) async-start(bf16[128,8,128]{2,1,0:T(8,128)(2,1)} %broadcast_in_dim.18), calls=%async_computation.1 | async-start | bytes 524288 | tf_op jit(solution)/shard_map/all_to_all | solution.py:368
  129.8 10.0 %all-to-all-done.1 = bf16[128,8,128]{2,1,0:T(8,128)(2,1)S(1)} async-done(((bf16[128,8,128]{2,1,0:T(8,128)(2,1)}), bf16[128,8,128]{2,1,0:T(8,128)(2,1)S(1)}, u32[]{:S(2)}, u32[]{:S(2)}) %all-to-all-start.1) | async-done | bytes 262176 | tf_op jit(solution)/shard_map/all_to_all | solution.py:368
  (88 shorter events, 26.0 us)
Async XLA Ops:
  3.4 14.7 %collective-permute-start = (s32[1,17]{1,0:T(1,128)S(1)}, s32[1,17]{1,0:T(1,128)S(1)}, u32[]{:S(2)}, u32[]{:S(2)}) collective-permute-start(s32[1,17]{1,0:T(1,128)S(1)} %pad_add_fusion.3), channel_id=1, source_target_pairs={{0,4},{4,8},{8,12},{12,0},{1,5},{5,9},{9,13},{13,1},{2,6},{6,10},{... | collective-permute-start | bytes 212 | tf_op jit(solution)/shard_map/ppermute | solution.py:269
  5.6 13.7 %collective-permute-start.1 = (s32[1,17]{1,0:T(1,128)S(1)}, s32[1,17]{1,0:T(1,128)S(1)}, u32[]{:S(2)}, u32[]{:S(2)}) collective-permute-start(s32[1,17]{1,0:T(1,128)S(1)} %pad_add_fusion.3), channel_id=1, source_target_pairs={{0,8},{4,12},{8,0},{12,4},{1,9},{5,13},{9,1},{13,5},{2,10},{6,14},... | collective-permute-start | bytes 212 | tf_op jit(solution)/shard_map/ppermute | solution.py:269
  8.2 6.4 %collective-permute-start.3 = (bf16[4,128,128]{2,1,0:T(8,128)(2,1)S(1)}, bf16[4,128,128]{2,1,0:T(8,128)(2,1)S(1)}, u32[]{:S(2)}, u32[]{:S(2)}) collective-permute-start(bf16[4,128,128]{2,1,0:T(8,128)(2,1)S(1)} %bitcast.75), channel_id=1, source_target_pairs={{0,1},{1,2},{2,3},{3,0},{4,5},{5,6},{6,7},{7,4},{8,9},{9,10},{10,1... | collective-permute-start | bytes 393224 | tf_op jit(solution)/shard_map/ppermute | solution.py:269
  9.4 15.3 %collective-permute-start.7 = (bf16[4,128,128]{2,1,0:T(8,128)(2,1)S(1)}, bf16[4,128,128]{2,1,0:T(8,128)(2,1)S(1)}, u32[]{:S(2)}, u32[]{:S(2)}) collective-permute-start(bf16[4,128,128]{2,1,0:T(8,128)(2,1)S(1)} %bitcast.76), channel_id=1, source_target_pairs={{0,2},{1,3},{2,0},{3,1},{4,6},{5,7},{6,4},{7,5},{8,10},{9,11},{10,... | collective-permute-start | bytes 393224 | tf_op jit(solution)/shard_map/ppermute | solution.py:269
  11.8 12.8 %collective-permute-start.8 = (bf16[4,128,128]{2,1,0:T(8,128)(2,1)S(1)}, bf16[4,128,128]{2,1,0:T(8,128)(2,1)S(1)}, u32[]{:S(2)}, u32[]{:S(2)}) collective-permute-start(bf16[4,128,128]{2,1,0:T(8,128)(2,1)S(1)} %bitcast.77), channel_id=1, source_target_pairs={{0,3},{1,0},{2,1},{3,2},{4,7},{5,4},{6,5},{7,6},{8,11},{9,8},{10,9... | collective-permute-start | bytes 393224 | tf_op jit(solution)/shard_map/ppermute | solution.py:269
  16.4 11.6 %collective-permute-start.4 = (bf16[4,128,128]{2,1,0:T(8,128)(2,1)}, bf16[4,128,128]{2,1,0:T(8,128)(2,1)S(1)}, u32[]{:S(2)}, u32[]{:S(2)}) collective-permute-start(bf16[4,128,128]{2,1,0:T(8,128)(2,1)} %bitcast.8), channel_id=1, source_target_pairs={{0,32},{32,64},{64,96},{96,0},{1,33},{33,65},{65,97},{97,1},{2,34}... | collective-permute-start | bytes 393224 | tf_op jit(solution)/shard_map/ppermute | solution.py:269
  20.5 9.0 %collective-permute-start.5 = (bf16[4,128,128]{2,1,0:T(8,128)(2,1)}, bf16[4,128,128]{2,1,0:T(8,128)(2,1)S(1)}, u32[]{:S(2)}, u32[]{:S(2)}) collective-permute-start(bf16[4,128,128]{2,1,0:T(8,128)(2,1)} %bitcast.8), channel_id=1, source_target_pairs={{0,64},{32,96},{64,0},{96,32},{1,65},{33,97},{65,1},{97,33},{2,66}... | collective-permute-start | bytes 393224 | tf_op jit(solution)/shard_map/ppermute | solution.py:269
  23.9 5.6 %collective-permute-start.6 = (bf16[4,128,128]{2,1,0:T(8,128)(2,1)}, bf16[4,128,128]{2,1,0:T(8,128)(2,1)S(1)}, u32[]{:S(2)}, u32[]{:S(2)}) collective-permute-start(bf16[4,128,128]{2,1,0:T(8,128)(2,1)} %bitcast.8), channel_id=1, source_target_pairs={{0,96},{32,0},{64,32},{96,64},{1,97},{33,1},{65,33},{97,65},{2,98}... | collective-permute-start | bytes 393224 | tf_op jit(solution)/shard_map/ppermute | solution.py:269
  25.6 6.9 %collective-permute-start.10 = (bf16[8,128,128]{2,1,0:T(8,128)(2,1)S(1)}, bf16[8,128,128]{2,1,0:T(8,128)(2,1)S(1)}, u32[]{:S(2)}, u32[]{:S(2)}) collective-permute-start(bf16[8,128,128]{2,1,0:T(8,128)(2,1)S(1)} %get-tuple-element.34), channel_id=1, source_target_pairs={{0,8},{4,12},{8,0},{12,4},{1,9},{5,13},{9,1},{13,5},{2,10},{6,14},... | collective-permute-start | bytes 786440 | tf_op jit(solution)/shard_map/ppermute | solution.py:269
  26.4 11.4 %collective-permute-start.11 = (bf16[8,128,128]{2,1,0:T(8,128)(2,1)S(1)}, bf16[8,128,128]{2,1,0:T(8,128)(2,1)S(1)}, u32[]{:S(2)}, u32[]{:S(2)}) collective-permute-start(bf16[8,128,128]{2,1,0:T(8,128)(2,1)S(1)} %get-tuple-element.35), channel_id=1, source_target_pairs={{0,12},{4,0},{8,4},{12,8},{1,13},{5,1},{9,5},{13,9},{2,14},{6,2},{... | collective-permute-start | bytes 786440 | tf_op jit(solution)/shard_map/ppermute | solution.py:269
  28.0 9.8 %collective-permute-start.9 = (bf16[8,128,128]{2,1,0:T(8,128)(2,1)S(1)}, bf16[8,128,128]{2,1,0:T(8,128)(2,1)S(1)}, u32[]{:S(2)}, u32[]{:S(2)}) collective-permute-start(bf16[8,128,128]{2,1,0:T(8,128)(2,1)S(1)} %get-tuple-element.33), channel_id=1, source_target_pairs={{0,4},{4,8},{8,12},{12,0},{1,5},{5,9},{9,13},{13,1},{2,6},{6,10},{... | collective-permute-start | bytes 786440 | tf_op jit(solution)/shard_map/ppermute | solution.py:269
  38.0 5.2 %collective-permute-start.12 = (bf16[2064,128]{1,0:T(8,128)(2,1)S(1)}, bf16[2064,128]{1,0:T(8,128)(2,1)S(1)}, u32[]{:S(2)}, u32[]{:S(2)}) collective-permute-start(bf16[2064,128]{1,0:T(8,128)(2,1)S(1)} %constant_dynamic-update-slice_fusion.right0), channel_id=1, source_target_pairs={{0,16},{16,0},{1,17},{17,1},{2,18},{18,2},{3,19},{19,3},{4,20},{20... | collective-permute-start | bytes 1585160 | tf_op jit(solution)/shard_map/ppermute | solution.py:269
  53.9 23.6 %collective-permute-start.16 = (bf16[8,128,128]{2,1,0:T(8,128)(2,1)S(1)}, bf16[8,128,128]{2,1,0:T(8,128)(2,1)S(1)}, u32[]{:S(2)}, u32[]{:S(2)}) collective-permute-start(bf16[8,128,128]{2,1,0:T(8,128)(2,1)S(1)} %get-tuple-element.41.refs_0_), channel_id=1, source_target_pairs={{0,16},{16,0},{1,17},{17,1},{2,18},{18,2},{3,19},{19,3},{4,20},{20... | collective-permute-start | bytes 786440 | tf_op jit(solution)/shard_map/ppermute | solution.py:269
  58.4 21.1 %collective-permute-start.13 = (bf16[8,128,128]{2,1,0:T(8,128)(2,1)S(1)}, bf16[8,128,128]{2,1,0:T(8,128)(2,1)S(1)}, u32[]{:S(2)}, u32[]{:S(2)}) collective-permute-start(bf16[8,128,128]{2,1,0:T(8,128)(2,1)S(1)} %get-tuple-element.40.refs_0_), channel_id=1, source_target_pairs={{0,4},{4,8},{8,12},{12,0},{1,5},{5,9},{9,13},{13,1},{2,6},{6,10},{... | collective-permute-start | bytes 786440 | tf_op jit(solution)/shard_map/ppermute | solution.py:269
  58.4 29.1 %collective-permute-start.14 = (bf16[8,128,128]{2,1,0:T(8,128)(2,1)S(1)}, bf16[8,128,128]{2,1,0:T(8,128)(2,1)S(1)}, u32[]{:S(2)}, u32[]{:S(2)}) collective-permute-start(bf16[8,128,128]{2,1,0:T(8,128)(2,1)S(1)} %get-tuple-element.40.refs_0_), channel_id=1, source_target_pairs={{0,8},{4,12},{8,0},{12,4},{1,9},{5,13},{9,1},{13,5},{2,10},{6,14},... | collective-permute-start | bytes 786440 | tf_op jit(solution)/shard_map/ppermute | solution.py:269
  75.4 12.1 %collective-permute-start.15 = (bf16[8,128,128]{2,1,0:T(8,128)(2,1)S(1)}, bf16[8,128,128]{2,1,0:T(8,128)(2,1)S(1)}, u32[]{:S(2)}, u32[]{:S(2)}) collective-permute-start(bf16[8,128,128]{2,1,0:T(8,128)(2,1)S(1)} %get-tuple-element.40.refs_0_), channel_id=1, source_target_pairs={{0,12},{4,0},{8,4},{12,8},{1,13},{5,1},{9,5},{13,9},{2,14},{6,2},{... | collective-permute-start | bytes 786440 | tf_op jit(solution)/shard_map/ppermute | solution.py:269
  78.3 9.2 %collective-permute-start.17 = (bf16[4,128,128]{2,1,0:T(8,128)(2,1)S(1)}, bf16[4,128,128]{2,1,0:T(8,128)(2,1)S(1)}, u32[]{:S(2)}, u32[]{:S(2)}) collective-permute-start(bf16[4,128,128]{2,1,0:T(8,128)(2,1)S(1)} %get-tuple-element.42), channel_id=1, source_target_pairs={{0,32},{32,64},{64,96},{96,0},{1,33},{33,65},{65,97},{97,1},{2,34}... | collective-permute-start | bytes 393224 | tf_op jit(solution)/shard_map/ppermute | solution.py:269
  79.5 8.0 %collective-permute-start.18 = (bf16[4,128,128]{2,1,0:T(8,128)(2,1)S(1)}, bf16[4,128,128]{2,1,0:T(8,128)(2,1)S(1)}, u32[]{:S(2)}, u32[]{:S(2)}) collective-permute-start(bf16[4,128,128]{2,1,0:T(8,128)(2,1)S(1)} %get-tuple-element.43), channel_id=1, source_target_pairs={{0,64},{32,96},{64,0},{96,32},{1,65},{33,97},{65,1},{97,33},{2,66}... | collective-permute-start | bytes 393224 | tf_op jit(solution)/shard_map/ppermute | solution.py:269
  79.5 8.5 %collective-permute-start.19 = (bf16[4,128,128]{2,1,0:T(8,128)(2,1)S(1)}, bf16[4,128,128]{2,1,0:T(8,128)(2,1)S(1)}, u32[]{:S(2)}, u32[]{:S(2)}) collective-permute-start(bf16[4,128,128]{2,1,0:T(8,128)(2,1)S(1)} %get-tuple-element.44), channel_id=1, source_target_pairs={{0,96},{32,0},{64,32},{96,64},{1,97},{33,1},{65,33},{97,65},{2,98}... | collective-permute-start | bytes 393224 | tf_op jit(solution)/shard_map/ppermute | solution.py:269
  89.3 8.6 %collective-permute-start.20 = (bf16[4,128,128]{2,1,0:T(8,128)(2,1)S(1)}, bf16[4,128,128]{2,1,0:T(8,128)(2,1)S(1)}, u32[]{:S(2)}, u32[]{:S(2)}) collective-permute-start(bf16[4,128,128]{2,1,0:T(8,128)(2,1)S(1)} %get-tuple-element.49), channel_id=1, source_target_pairs={{0,1},{1,2},{2,3},{3,0},{4,5},{5,6},{6,7},{7,4},{8,9},{9,10},{10,1... | collective-permute-start | bytes 393224 | tf_op jit(solution)/shard_map/ppermute | solution.py:269
  95.0 5.5 %collective-permute-start.21 = (bf16[4,128,128]{2,1,0:T(8,128)(2,1)S(1)}, bf16[4,128,128]{2,1,0:T(8,128)(2,1)S(1)}, u32[]{:S(2)}, u32[]{:S(2)}) collective-permute-start(bf16[4,128,128]{2,1,0:T(8,128)(2,1)S(1)} %get-tuple-element.50), channel_id=1, source_target_pairs={{0,2},{1,3},{2,0},{3,1},{4,6},{5,7},{6,4},{7,5},{8,10},{9,11},{10,... | collective-permute-start | bytes 393224 | tf_op jit(solution)/shard_map/ppermute | solution.py:269
  95.4 5.5 %collective-permute-start.22 = (bf16[4,128,128]{2,1,0:T(8,128)(2,1)S(1)}, bf16[4,128,128]{2,1,0:T(8,128)(2,1)S(1)}, u32[]{:S(2)}, u32[]{:S(2)}) collective-permute-start(bf16[4,128,128]{2,1,0:T(8,128)(2,1)S(1)} %get-tuple-element.51), channel_id=1, source_target_pairs={{0,3},{1,0},{2,1},{3,2},{4,7},{5,4},{6,5},{7,6},{8,11},{9,8},{10,9... | collective-permute-start | bytes 393224 | tf_op jit(solution)/shard_map/ppermute | solution.py:269
  102.5 21.0 %all-to-all-start = ((bf16[128,7,128]{2,1,0:T(8,128)(2,1)}), bf16[128,7,128]{2,1,0:T(8,128)(2,1)S(1)}, u32[]{:S(2)}, u32[]{:S(2)}) async-start(bf16[128,7,128]{2,1,0:T(8,128)(2,1)} %reshape.122), calls=%async_computation | async-start | bytes 524288 | tf_op jit(solution)/shard_map/all_to_all | solution.py:365
  124.3 15.5 %all-to-all-start.1 = ((bf16[128,8,128]{2,1,0:T(8,128)(2,1)}), bf16[128,8,128]{2,1,0:T(8,128)(2,1)S(1)}, u32[]{:S(2)}, u32[]{:S(2)}) async-start(bf16[128,8,128]{2,1,0:T(8,128)(2,1)} %broadcast_in_dim.18), calls=%async_computation.1 | async-start | bytes 524288 | tf_op jit(solution)/shard_map/all_to_all | solution.py:368
  (5 other events, 193.6 us)

commit v3 on v2

--- a/solution.py
+++ b/solution.py
@@ -8,7 +8,7 @@
 from jax.sharding import PartitionSpec as P
 
 GROUP_SCORES = 64
-GROUP_SOFT = 16
+GROUP_SOFT = 64
 GROUP_GRADS = 64
 
 

time: 146 us -> 146 us (level)
  waiting for transfers between devices: 38.2 us -> 41.1 us
  starting transfers between devices: 72.5 us -> 70.5 us
    ppermute x23, waiting for transfers between devices: 17.4 us -> 20.3 us  [shift(): lax.ppermute(value, axis, [(i, (i + step) % size) for i in range(size)])]
    all_to_all x1, starting transfers between devices: 9.71 us -> 8.19 us  [per_device(): mine = jnp.sum(lax.all_to_all(packed, AXES, 0, 0).astype(f32), axis=0)]
where the time goes in v3:
time: 146 us
  starting transfers between devices  70.5 us (48%)
  waiting for transfers between devices  41.1 us (28%)
  Pallas kernels  12.8 us (9%)
  between operations  6.57 us (4%)
  local copies, waits for them, and re-layouts  5.99 us (4%)
  matrix products  5.61 us (4%)
  other arithmetic  3.77 us (3%)
    ppermute x23, starting transfers between devices, shift(): lax.ppermute(value, axis, [(i, (i + step) % size) for i in range(size)])  58.1 us
    ppermute x23, waiting for transfers between devices, shift(): lax.ppermute(value, axis, [(i, (i + step) % size) for i in range(size)])  20.3 us
    all_to_all x1, waiting for transfers between devices, per_device(): mine = jnp.sum(lax.all_to_all(packed, AXES, 0, 0).astype(f32), axis=0)  10.8 us
    all_to_all x1, waiting for transfers between devices, per_device(): lax.all_to_all(jnp.broadcast_to(mine[None], (devices, chunk + 1, width)),...  10 us
    pallas_call x1, Pallas kernels, run_blocks(): pl.pallas_call(blocks_kernel, out_shape=[piece] * 2 + [jax.ShapeDtypeStru...  9.72 us
    all_to_all x1, starting transfers between devices, per_device(): mine = jnp.sum(lax.all_to_all(packed, AXES, 0, 0).astype(f32), axis=0)  8.19 us
    all_to_all x1, starting transfers between devices, per_device(): lax.all_to_all(jnp.broadcast_to(mine[None], (devices, chunk + 1, width)),...  4.2 us
  transfers between devices with their start and end apart: 25, of which 10 were waited for; matrix products, arithmetic and copies ran while one was open for 5% of the time, Pallas kernels for 1%

profile of v3, /device:TPU:1, one launch (start us, length us, event | category | flops | bytes accessed | tf_op | source)
XLA Modules:
  0.0 146.3 jit_solution(10608532503839940595)
XLA Ops:
  3.4 2.1 %collective-permute-start = (s32[1,17]{1,0:T(1,128)S(1)}, s32[1,17]{1,0:T(1,128)S(1)}, u32[]{:S(2)}, u32[]{:S(2)}) collective-permute-start(s32[1,17]{1,0:T(1,128)S(1)} %pad_add_fusion.3), channel_id=1, source_target_pairs={{0,4},{4,8},{8,12},{12,0},{1,5},{5,9},{9,13},{13,1},{2,6},{6,10},{... | collective-permute-start | bytes 212 | tf_op jit(solution)/shard_map/ppermute | solution.py:269
  5.6 2.6 %collective-permute-start.1 = (s32[1,17]{1,0:T(1,128)S(1)}, s32[1,17]{1,0:T(1,128)S(1)}, u32[]{:S(2)}, u32[]{:S(2)}) collective-permute-start(s32[1,17]{1,0:T(1,128)S(1)} %pad_add_fusion.3), channel_id=1, source_target_pairs={{0,8},{4,12},{8,0},{12,4},{1,9},{5,13},{9,1},{13,5},{2,10},{6,14},... | collective-permute-start | bytes 212 | tf_op jit(solution)/shard_map/ppermute | solution.py:269
  9.4 2.4 %collective-permute-start.7 = (bf16[4,128,128]{2,1,0:T(8,128)(2,1)S(1)}, bf16[4,128,128]{2,1,0:T(8,128)(2,1)S(1)}, u32[]{:S(2)}, u32[]{:S(2)}) collective-permute-start(bf16[4,128,128]{2,1,0:T(8,128)(2,1)S(1)} %bitcast.76), channel_id=1, source_target_pairs={{0,2},{1,3},{2,0},{3,1},{4,6},{5,7},{6,4},{7,5},{8,10},{9,11},{10,... | collective-permute-start | bytes 393224 | tf_op jit(solution)/shard_map/ppermute | solution.py:269
  14.6 1.8 %constant_dynamic-update-slice_fusion.4 = (bf16[2064,128]{1,0:T(8,128)(2,1)S(1)}, bf16[512,128]{1,0:T(8,128)(2,1)}) fusion(bf16[512,384]{1,0:T(8,128)(2,1)S(1)} %copy-done, bf16[384,128]{1,0:T(8,128)(2,1)} %param.10), kind=kOutput, calls=%fused_computation.23 | convolution fusion | flops 50397184 | bytes 753664 | tf_op jit(solution)/shard_map/dot_general | solution.py:305
  16.4 1.6 %collective-permute-start.4 = (bf16[4,128,128]{2,1,0:T(8,128)(2,1)}, bf16[4,128,128]{2,1,0:T(8,128)(2,1)S(1)}, u32[]{:S(2)}, u32[]{:S(2)}) collective-permute-start(bf16[4,128,128]{2,1,0:T(8,128)(2,1)} %bitcast.8), channel_id=1, source_target_pairs={{0,32},{32,64},{64,96},{96,0},{1,33},{33,65},{65,97},{97,1},{2,34}... | collective-permute-start | bytes 393224 | tf_op jit(solution)/shard_map/ppermute | solution.py:269
  20.5 3.4 %collective-permute-start.5 = (bf16[4,128,128]{2,1,0:T(8,128)(2,1)}, bf16[4,128,128]{2,1,0:T(8,128)(2,1)S(1)}, u32[]{:S(2)}, u32[]{:S(2)}) collective-permute-start(bf16[4,128,128]{2,1,0:T(8,128)(2,1)} %bitcast.8), channel_id=1, source_target_pairs={{0,64},{32,96},{64,0},{96,32},{1,65},{33,97},{65,1},{97,33},{2,66}... | collective-permute-start | bytes 393224 | tf_op jit(solution)/shard_map/ppermute | solution.py:269
  26.4 1.6 %collective-permute-start.11 = (bf16[8,128,128]{2,1,0:T(8,128)(2,1)S(1)}, bf16[8,128,128]{2,1,0:T(8,128)(2,1)S(1)}, u32[]{:S(2)}, u32[]{:S(2)}) collective-permute-start(bf16[8,128,128]{2,1,0:T(8,128)(2,1)S(1)} %get-tuple-element.35), channel_id=1, source_target_pairs={{0,12},{4,0},{8,4},{12,8},{1,13},{5,1},{9,5},{13,9},{2,14},{6,2},{... | collective-permute-start | bytes 786440 | tf_op jit(solution)/shard_map/ppermute | solution.py:269
  29.6 2.9 %collective-permute-done.10.left2 = bf16[8,128,128]{2,1,0:T(8,128)(2,1)S(1)} collective-permute-done((bf16[8,128,128]{2,1,0:T(8,128)(2,1)S(1)}, bf16[8,128,128]{2,1,0:T(8,128)(2,1)S(1)}, u32[]{:S(2)}, u32[]{:S(2)}) %collective-permute-start.10) | collective-permute-done | bytes 262176 | tf_op jit(solution)/shard_map/ppermute | solution.py:269
  32.4 5.4 %collective-permute-done.11.left3 = bf16[8,128,128]{2,1,0:T(8,128)(2,1)S(1)} collective-permute-done((bf16[8,128,128]{2,1,0:T(8,128)(2,1)S(1)}, bf16[8,128,128]{2,1,0:T(8,128)(2,1)S(1)}, u32[]{:S(2)}, u32[]{:S(2)}) %collective-permute-start.11) | collective-permute-done | bytes 262176 | tf_op jit(solution)/shard_map/ppermute | solution.py:269
  38.0 3.7 %collective-permute-start.12 = (bf16[2064,128]{1,0:T(8,128)(2,1)S(1)}, bf16[2064,128]{1,0:T(8,128)(2,1)S(1)}, u32[]{:S(2)}, u32[]{:S(2)}) collective-permute-start(bf16[2064,128]{1,0:T(8,128)(2,1)S(1)} %constant_dynamic-update-slice_fusion.right0), channel_id=1, source_target_pairs={{0,16},{16,0},{1,17},{17,1},{2,18},{18,2},{3,19},{19,3},{4,20},{20... | collective-permute-start | bytes 1585160 | tf_op jit(solution)/shard_map/ppermute | solution.py:269
  41.8 1.4 collective-permute-done.12.right1
  43.9 9.7 %shard_map.120 = (bf16[8,128,128]{2,1,0:T(8,128)(2,1)S(1)}, bf16[8,128,128]{2,1,0:T(8,128)(2,1)S(1)}, f32[64,8,128]{2,1,0:T(8,128)S(1)}, f32[8,128]{1,0:T(8,128)S(1)}) custom-call(s32[8,3]{1,0:T(8,128)S(1)} %pad_add_fusion.place, s32[1]{0:T(128)} %copy.49.count, f32[64]{0:T(128)S(1)} %copy-done.1, f32[64,128]{1,0:T(8,128)S(1)} %copy.38.w_turned, ...), custom_call_target="tpu_custom_call" | custom-call | flops 6442450944 | bytes 20971520 | tf_op jit(solution)/shard_map/pallas_call | solution.py:162
  53.7 11.7 %collective-permute-start.13 = (bf16[8,128,128]{2,1,0:T(8,128)(2,1)S(1)}, bf16[8,128,128]{2,1,0:T(8,128)(2,1)S(1)}, u32[]{:S(2)}, u32[]{:S(2)}) collective-permute-start(bf16[8,128,128]{2,1,0:T(8,128)(2,1)S(1)} %get-tuple-element.40.refs_0_), channel_id=1, source_target_pairs={{0,4},{4,8},{8,12},{12,0},{1,5},{5,9},{9,13},{13,1},{2,6},{6,10},{... | collective-permute-start | bytes 786440 | tf_op jit(solution)/shard_map/ppermute | solution.py:269
  65.4 7.6 %collective-permute-start.14 = (bf16[8,128,128]{2,1,0:T(8,128)(2,1)S(1)}, bf16[8,128,128]{2,1,0:T(8,128)(2,1)S(1)}, u32[]{:S(2)}, u32[]{:S(2)}) collective-permute-start(bf16[8,128,128]{2,1,0:T(8,128)(2,1)S(1)} %get-tuple-element.40.refs_0_), channel_id=1, source_target_pairs={{0,8},{4,12},{8,0},{12,4},{1,9},{5,13},{9,1},{13,5},{2,10},{6,14},... | collective-permute-start | bytes 786440 | tf_op jit(solution)/shard_map/ppermute | solution.py:269
  74.1 3.9 %collective-permute-start.18 = (bf16[4,128,128]{2,1,0:T(8,128)(2,1)S(1)}, bf16[4,128,128]{2,1,0:T(8,128)(2,1)S(1)}, u32[]{:S(2)}, u32[]{:S(2)}) collective-permute-start(bf16[4,128,128]{2,1,0:T(8,128)(2,1)S(1)} %get-tuple-element.43), channel_id=1, source_target_pairs={{0,64},{32,96},{64,0},{96,32},{1,65},{33,97},{65,1},{97,33},{2,66}... | collective-permute-start | bytes 393224 | tf_op jit(solution)/shard_map/ppermute | solution.py:269
  81.5 3.4 %collective-permute-done.14.refs_2_ = bf16[8,128,128]{2,1,0:T(8,128)(2,1)S(1)} collective-permute-done((bf16[8,128,128]{2,1,0:T(8,128)(2,1)S(1)}, bf16[8,128,128]{2,1,0:T(8,128)(2,1)S(1)}, u32[]{:S(2)}, u32[]{:S(2)}) %collective-permute-start.14) | collective-permute-done | bytes 262176 | tf_op jit(solution)/shard_map/ppermute | solution.py:269
  84.9 3.3 %collective-permute-done.19 = bf16[4,128,128]{2,1,0:T(8,128)(2,1)S(1)} collective-permute-done((bf16[4,128,128]{2,1,0:T(8,128)(2,1)S(1)}, bf16[4,128,128]{2,1,0:T(8,128)(2,1)S(1)}, u32[]{:S(2)}, u32[]{:S(2)}) %collective-permute-start.19) | collective-permute-done | bytes 131104 | tf_op jit(solution)/shard_map/ppermute | solution.py:269
  89.5 8.2 %collective-permute-start.20 = (bf16[4,128,128]{2,1,0:T(8,128)(2,1)S(1)}, bf16[4,128,128]{2,1,0:T(8,128)(2,1)S(1)}, u32[]{:S(2)}, u32[]{:S(2)}) collective-permute-start(bf16[4,128,128]{2,1,0:T(8,128)(2,1)S(1)} %get-tuple-element.49), channel_id=1, source_target_pairs={{0,1},{1,2},{2,3},{3,0},{4,5},{5,6},{6,7},{7,4},{8,9},{9,10},{10,1... | collective-permute-start | bytes 393224 | tf_op jit(solution)/shard_map/ppermute | solution.py:269
  97.7 2.5 %collective-permute-start.22 = (bf16[4,128,128]{2,1,0:T(8,128)(2,1)S(1)}, bf16[4,128,128]{2,1,0:T(8,128)(2,1)S(1)}, u32[]{:S(2)}, u32[]{:S(2)}) collective-permute-start(bf16[4,128,128]{2,1,0:T(8,128)(2,1)S(1)} %get-tuple-element.51), channel_id=1, source_target_pairs={{0,3},{1,0},{2,1},{3,2},{4,7},{5,4},{6,5},{7,6},{8,11},{9,8},{10,9... | collective-permute-start | bytes 393224 | tf_op jit(solution)/shard_map/ppermute | solution.py:269
  100.8 2.3 %collective-permute-done.21 = bf16[4,128,128]{2,1,0:T(8,128)(2,1)S(1)} collective-permute-done((bf16[4,128,128]{2,1,0:T(8,128)(2,1)S(1)}, bf16[4,128,128]{2,1,0:T(8,128)(2,1)S(1)}, u32[]{:S(2)}, u32[]{:S(2)}) %collective-permute-start.21) | collective-permute-done | bytes 131104 | tf_op jit(solution)/shard_map/ppermute | solution.py:269
  104.6 8.2 %all-to-all-start = ((bf16[128,7,128]{2,1,0:T(8,128)(2,1)}), bf16[128,7,128]{2,1,0:T(8,128)(2,1)S(1)}, u32[]{:S(2)}, u32[]{:S(2)}) async-start(bf16[128,7,128]{2,1,0:T(8,128)(2,1)} %reshape.122), calls=%async_computation | async-start | bytes 524288 | tf_op jit(solution)/shard_map/all_to_all | solution.py:365
  113.3 10.8 %all-to-all-done = bf16[128,7,128]{2,1,0:T(8,128)(2,1)S(1)} async-done(((bf16[128,7,128]{2,1,0:T(8,128)(2,1)}), bf16[128,7,128]{2,1,0:T(8,128)(2,1)S(1)}, u32[]{:S(2)}, u32[]{:S(2)}) %all-to-all-start) | async-done | bytes 229408 | tf_op jit(solution)/shard_map/all_to_all | solution.py:365
  125.0 4.2 %all-to-all-start.1 = ((bf16[128,8,128]{2,1,0:T(8,128)(2,1)}), bf16[128,8,128]{2,1,0:T(8,128)(2,1)S(1)}, u32[]{:S(2)}, u32[]{:S(2)}) async-start(bf16[128,8,128]{2,1,0:T(8,128)(2,1)} %broadcast_in_dim.18), calls=%async_computation.1 | async-start | bytes 524288 | tf_op jit(solution)/shard_map/all_to_all | solution.py:368
  130.5 10.0 %all-to-all-done.1 = bf16[128,8,128]{2,1,0:T(8,128)(2,1)S(1)} async-done(((bf16[128,8,128]{2,1,0:T(8,128)(2,1)}), bf16[128,8,128]{2,1,0:T(8,128)(2,1)S(1)}, u32[]{:S(2)}, u32[]{:S(2)}) %all-to-all-start.1) | async-done | bytes 262176 | tf_op jit(solution)/shard_map/all_to_all | solution.py:368
  (88 shorter events, 25.0 us)
Async XLA Ops:
  3.4 14.7 %collective-permute-start = (s32[1,17]{1,0:T(1,128)S(1)}, s32[1,17]{1,0:T(1,128)S(1)}, u32[]{:S(2)}, u32[]{:S(2)}) collective-permute-start(s32[1,17]{1,0:T(1,128)S(1)} %pad_add_fusion.3), channel_id=1, source_target_pairs={{0,4},{4,8},{8,12},{12,0},{1,5},{5,9},{9,13},{13,1},{2,6},{6,10},{... | collective-permute-start | bytes 212 | tf_op jit(solution)/shard_map/ppermute | solution.py:269
  5.6 13.7 %collective-permute-start.1 = (s32[1,17]{1,0:T(1,128)S(1)}, s32[1,17]{1,0:T(1,128)S(1)}, u32[]{:S(2)}, u32[]{:S(2)}) collective-permute-start(s32[1,17]{1,0:T(1,128)S(1)} %pad_add_fusion.3), channel_id=1, source_target_pairs={{0,8},{4,12},{8,0},{12,4},{1,9},{5,13},{9,1},{13,5},{2,10},{6,14},... | collective-permute-start | bytes 212 | tf_op jit(solution)/shard_map/ppermute | solution.py:269
  8.2 6.4 %collective-permute-start.3 = (bf16[4,128,128]{2,1,0:T(8,128)(2,1)S(1)}, bf16[4,128,128]{2,1,0:T(8,128)(2,1)S(1)}, u32[]{:S(2)}, u32[]{:S(2)}) collective-permute-start(bf16[4,128,128]{2,1,0:T(8,128)(2,1)S(1)} %bitcast.75), channel_id=1, source_target_pairs={{0,1},{1,2},{2,3},{3,0},{4,5},{5,6},{6,7},{7,4},{8,9},{9,10},{10,1... | collective-permute-start | bytes 393224 | tf_op jit(solution)/shard_map/ppermute | solution.py:269
  9.4 15.3 %collective-permute-start.7 = (bf16[4,128,128]{2,1,0:T(8,128)(2,1)S(1)}, bf16[4,128,128]{2,1,0:T(8,128)(2,1)S(1)}, u32[]{:S(2)}, u32[]{:S(2)}) collective-permute-start(bf16[4,128,128]{2,1,0:T(8,128)(2,1)S(1)} %bitcast.76), channel_id=1, source_target_pairs={{0,2},{1,3},{2,0},{3,1},{4,6},{5,7},{6,4},{7,5},{8,10},{9,11},{10,... | collective-permute-start | bytes 393224 | tf_op jit(solution)/shard_map/ppermute | solution.py:269
  11.8 12.8 %collective-permute-start.8 = (bf16[4,128,128]{2,1,0:T(8,128)(2,1)S(1)}, bf16[4,128,128]{2,1,0:T(8,128)(2,1)S(1)}, u32[]{:S(2)}, u32[]{:S(2)}) collective-permute-start(bf16[4,128,128]{2,1,0:T(8,128)(2,1)S(1)} %bitcast.77), channel_id=1, source_target_pairs={{0,3},{1,0},{2,1},{3,2},{4,7},{5,4},{6,5},{7,6},{8,11},{9,8},{10,9... | collective-permute-start | bytes 393224 | tf_op jit(solution)/shard_map/ppermute | solution.py:269
  16.4 11.6 %collective-permute-start.4 = (bf16[4,128,128]{2,1,0:T(8,128)(2,1)}, bf16[4,128,128]{2,1,0:T(8,128)(2,1)S(1)}, u32[]{:S(2)}, u32[]{:S(2)}) collective-permute-start(bf16[4,128,128]{2,1,0:T(8,128)(2,1)} %bitcast.8), channel_id=1, source_target_pairs={{0,32},{32,64},{64,96},{96,0},{1,33},{33,65},{65,97},{97,1},{2,34}... | collective-permute-start | bytes 393224 | tf_op jit(solution)/shard_map/ppermute | solution.py:269
  20.5 9.0 %collective-permute-start.5 = (bf16[4,128,128]{2,1,0:T(8,128)(2,1)}, bf16[4,128,128]{2,1,0:T(8,128)(2,1)S(1)}, u32[]{:S(2)}, u32[]{:S(2)}) collective-permute-start(bf16[4,128,128]{2,1,0:T(8,128)(2,1)} %bitcast.8), channel_id=1, source_target_pairs={{0,64},{32,96},{64,0},{96,32},{1,65},{33,97},{65,1},{97,33},{2,66}... | collective-permute-start | bytes 393224 | tf_op jit(solution)/shard_map/ppermute | solution.py:269
  23.9 5.6 %collective-permute-start.6 = (bf16[4,128,128]{2,1,0:T(8,128)(2,1)}, bf16[4,128,128]{2,1,0:T(8,128)(2,1)S(1)}, u32[]{:S(2)}, u32[]{:S(2)}) collective-permute-start(bf16[4,128,128]{2,1,0:T(8,128)(2,1)} %bitcast.8), channel_id=1, source_target_pairs={{0,96},{32,0},{64,32},{96,64},{1,97},{33,1},{65,33},{97,65},{2,98}... | collective-permute-start | bytes 393224 | tf_op jit(solution)/shard_map/ppermute | solution.py:269
  25.6 6.9 %collective-permute-start.10 = (bf16[8,128,128]{2,1,0:T(8,128)(2,1)S(1)}, bf16[8,128,128]{2,1,0:T(8,128)(2,1)S(1)}, u32[]{:S(2)}, u32[]{:S(2)}) collective-permute-start(bf16[8,128,128]{2,1,0:T(8,128)(2,1)S(1)} %get-tuple-element.34), channel_id=1, source_target_pairs={{0,8},{4,12},{8,0},{12,4},{1,9},{5,13},{9,1},{13,5},{2,10},{6,14},... | collective-permute-start | bytes 786440 | tf_op jit(solution)/shard_map/ppermute | solution.py:269
  26.4 11.4 %collective-permute-start.11 = (bf16[8,128,128]{2,1,0:T(8,128)(2,1)S(1)}, bf16[8,128,128]{2,1,0:T(8,128)(2,1)S(1)}, u32[]{:S(2)}, u32[]{:S(2)}) collective-permute-start(bf16[8,128,128]{2,1,0:T(8,128)(2,1)S(1)} %get-tuple-element.35), channel_id=1, source_target_pairs={{0,12},{4,0},{8,4},{12,8},{1,13},{5,1},{9,5},{13,9},{2,14},{6,2},{... | collective-permute-start | bytes 786440 | tf_op jit(solution)/shard_map/ppermute | solution.py:269
  28.0 9.8 %collective-permute-start.9 = (bf16[8,128,128]{2,1,0:T(8,128)(2,1)S(1)}, bf16[8,128,128]{2,1,0:T(8,128)(2,1)S(1)}, u32[]{:S(2)}, u32[]{:S(2)}) collective-permute-start(bf16[8,128,128]{2,1,0:T(8,128)(2,1)S(1)} %get-tuple-element.33), channel_id=1, source_target_pairs={{0,4},{4,8},{8,12},{12,0},{1,5},{5,9},{9,13},{13,1},{2,6},{6,10},{... | collective-permute-start | bytes 786440 | tf_op jit(solution)/shard_map/ppermute | solution.py:269
  38.0 5.2 %collective-permute-start.12 = (bf16[2064,128]{1,0:T(8,128)(2,1)S(1)}, bf16[2064,128]{1,0:T(8,128)(2,1)S(1)}, u32[]{:S(2)}, u32[]{:S(2)}) collective-permute-start(bf16[2064,128]{1,0:T(8,128)(2,1)S(1)} %constant_dynamic-update-slice_fusion.right0), channel_id=1, source_target_pairs={{0,16},{16,0},{1,17},{17,1},{2,18},{18,2},{3,19},{19,3},{4,20},{20... | collective-permute-start | bytes 1585160 | tf_op jit(solution)/shard_map/ppermute | solution.py:269
  53.6 19.4 %collective-permute-start.16 = (bf16[8,128,128]{2,1,0:T(8,128)(2,1)S(1)}, bf16[8,128,128]{2,1,0:T(8,128)(2,1)S(1)}, u32[]{:S(2)}, u32[]{:S(2)}) collective-permute-start(bf16[8,128,128]{2,1,0:T(8,128)(2,1)S(1)} %get-tuple-element.41.refs_0_), channel_id=1, source_target_pairs={{0,16},{16,0},{1,17},{17,1},{2,18},{18,2},{3,19},{19,3},{4,20},{20... | collective-permute-start | bytes 786440 | tf_op jit(solution)/shard_map/ppermute | solution.py:269
  53.7 24.6 %collective-permute-start.13 = (bf16[8,128,128]{2,1,0:T(8,128)(2,1)S(1)}, bf16[8,128,128]{2,1,0:T(8,128)(2,1)S(1)}, u32[]{:S(2)}, u32[]{:S(2)}) collective-permute-start(bf16[8,128,128]{2,1,0:T(8,128)(2,1)S(1)} %get-tuple-element.40.refs_0_), channel_id=1, source_target_pairs={{0,4},{4,8},{8,12},{12,0},{1,5},{5,9},{9,13},{13,1},{2,6},{6,10},{... | collective-permute-start | bytes 786440 | tf_op jit(solution)/shard_map/ppermute | solution.py:269
  65.4 19.5 %collective-permute-start.14 = (bf16[8,128,128]{2,1,0:T(8,128)(2,1)S(1)}, bf16[8,128,128]{2,1,0:T(8,128)(2,1)S(1)}, u32[]{:S(2)}, u32[]{:S(2)}) collective-permute-start(bf16[8,128,128]{2,1,0:T(8,128)(2,1)S(1)} %get-tuple-element.40.refs_0_), channel_id=1, source_target_pairs={{0,8},{4,12},{8,0},{12,4},{1,9},{5,13},{9,1},{13,5},{2,10},{6,14},... | collective-permute-start | bytes 786440 | tf_op jit(solution)/shard_map/ppermute | solution.py:269
  73.0 11.9 %collective-permute-start.15 = (bf16[8,128,128]{2,1,0:T(8,128)(2,1)S(1)}, bf16[8,128,128]{2,1,0:T(8,128)(2,1)S(1)}, u32[]{:S(2)}, u32[]{:S(2)}) collective-permute-start(bf16[8,128,128]{2,1,0:T(8,128)(2,1)S(1)} %get-tuple-element.40.refs_0_), channel_id=1, source_target_pairs={{0,12},{4,0},{8,4},{12,8},{1,13},{5,1},{9,5},{13,9},{2,14},{6,2},{... | collective-permute-start | bytes 786440 | tf_op jit(solution)/shard_map/ppermute | solution.py:269
  73.8 11.1 %collective-permute-start.17 = (bf16[4,128,128]{2,1,0:T(8,128)(2,1)S(1)}, bf16[4,128,128]{2,1,0:T(8,128)(2,1)S(1)}, u32[]{:S(2)}, u32[]{:S(2)}) collective-permute-start(bf16[4,128,128]{2,1,0:T(8,128)(2,1)S(1)} %get-tuple-element.42), channel_id=1, source_target_pairs={{0,32},{32,64},{64,96},{96,0},{1,33},{33,65},{65,97},{97,1},{2,34}... | collective-permute-start | bytes 393224 | tf_op jit(solution)/shard_map/ppermute | solution.py:269
  74.1 10.8 %collective-permute-start.18 = (bf16[4,128,128]{2,1,0:T(8,128)(2,1)S(1)}, bf16[4,128,128]{2,1,0:T(8,128)(2,1)S(1)}, u32[]{:S(2)}, u32[]{:S(2)}) collective-permute-start(bf16[4,128,128]{2,1,0:T(8,128)(2,1)S(1)} %get-tuple-element.43), channel_id=1, source_target_pairs={{0,64},{32,96},{64,0},{96,32},{1,65},{33,97},{65,1},{97,33},{2,66}... | collective-permute-start | bytes 393224 | tf_op jit(solution)/shard_map/ppermute | solution.py:269
  78.4 9.8 %collective-permute-start.19 = (bf16[4,128,128]{2,1,0:T(8,128)(2,1)S(1)}, bf16[4,128,128]{2,1,0:T(8,128)(2,1)S(1)}, u32[]{:S(2)}, u32[]{:S(2)}) collective-permute-start(bf16[4,128,128]{2,1,0:T(8,128)(2,1)S(1)} %get-tuple-element.44), channel_id=1, source_target_pairs={{0,96},{32,0},{64,32},{96,64},{1,97},{33,1},{65,33},{97,65},{2,98}... | collective-permute-start | bytes 393224 | tf_op jit(solution)/shard_map/ppermute | solution.py:269
  89.5 11.2 %collective-permute-start.20 = (bf16[4,128,128]{2,1,0:T(8,128)(2,1)S(1)}, bf16[4,128,128]{2,1,0:T(8,128)(2,1)S(1)}, u32[]{:S(2)}, u32[]{:S(2)}) collective-permute-start(bf16[4,128,128]{2,1,0:T(8,128)(2,1)S(1)} %get-tuple-element.49), channel_id=1, source_target_pairs={{0,1},{1,2},{2,3},{3,0},{4,5},{5,6},{6,7},{7,4},{8,9},{9,10},{10,1... | collective-permute-start | bytes 393224 | tf_op jit(solution)/shard_map/ppermute | solution.py:269
  97.7 5.3 %collective-permute-start.21 = (bf16[4,128,128]{2,1,0:T(8,128)(2,1)S(1)}, bf16[4,128,128]{2,1,0:T(8,128)(2,1)S(1)}, u32[]{:S(2)}, u32[]{:S(2)}) collective-permute-start(bf16[4,128,128]{2,1,0:T(8,128)(2,1)S(1)} %get-tuple-element.50), channel_id=1, source_target_pairs={{0,2},{1,3},{2,0},{3,1},{4,6},{5,7},{6,4},{7,5},{8,10},{9,11},{10,... | collective-permute-start | bytes 393224 | tf_op jit(solution)/shard_map/ppermute | solution.py:269
  97.7 5.3 %collective-permute-start.22 = (bf16[4,128,128]{2,1,0:T(8,128)(2,1)S(1)}, bf16[4,128,128]{2,1,0:T(8,128)(2,1)S(1)}, u32[]{:S(2)}, u32[]{:S(2)}) collective-permute-start(bf16[4,128,128]{2,1,0:T(8,128)(2,1)S(1)} %get-tuple-element.51), channel_id=1, source_target_pairs={{0,3},{1,0},{2,1},{3,2},{4,7},{5,4},{6,5},{7,6},{8,11},{9,8},{10,9... | collective-permute-start | bytes 393224 | tf_op jit(solution)/shard_map/ppermute | solution.py:269
  104.6 19.5 %all-to-all-start = ((bf16[128,7,128]{2,1,0:T(8,128)(2,1)}), bf16[128,7,128]{2,1,0:T(8,128)(2,1)S(1)}, u32[]{:S(2)}, u32[]{:S(2)}) async-start(bf16[128,7,128]{2,1,0:T(8,128)(2,1)} %reshape.122), calls=%async_computation | async-start | bytes 524288 | tf_op jit(solution)/shard_map/all_to_all | solution.py:365
  125.0 15.5 %all-to-all-start.1 = ((bf16[128,8,128]{2,1,0:T(8,128)(2,1)}), bf16[128,8,128]{2,1,0:T(8,128)(2,1)S(1)}, u32[]{:S(2)}, u32[]{:S(2)}) async-start(bf16[128,8,128]{2,1,0:T(8,128)(2,1)} %broadcast_in_dim.18), calls=%async_computation.1 | async-start | bytes 524288 | tf_op jit(solution)/shard_map/all_to_all | solution.py:368
  (5 other events, 194.9 us)
